TPU v7x, 32 devices: a whole 2x2x4 slice. The times are simulated.
32 devices in a mesh: wide: 8 (over z, core), narrow: 4 (over y, x).
Axes of the slice: x: 2, y: 2, z: 4, core: 2. Of those that a mesh axis runs over, the one named last changes fastest.
Arguments:
- tokens: bfloat16 [32768, 768], P(('wide', 'narrow')), may hold values from -6 to 6
- cotangent: bfloat16 [32768, 768], P(('wide', 'narrow')), may hold values from -6 to 6
- bucket_counts: int32 [32, 3], P(('wide', 'narrow')), may hold values from 0 to 2, as said below
- attn_gain: bfloat16 [768], P(('wide', 'narrow')), may hold values from 0.5 to 1.5
- attn_shift: bfloat16 [768], P(('wide', 'narrow')), may hold values from -4 to 4
- dense_weight: bfloat16 [12, 768, 768], P(None, ('wide', 'narrow')), may hold values from -0.21875 to 0.21875
- dense_bias: bfloat16 [9216], P(('wide', 'narrow')), may hold values from -6 to 6
- logit_weight: bfloat16 [12, 768, 512], P(None, ('wide', 'narrow')), may hold values from -0.5 to 0.5
- logit_bias: bfloat16 [6144], P(('wide', 'narrow')), may hold values from -6 to 6
- value_weight: bfloat16 [768, 768], P(('wide', 'narrow')), may hold values from -0.21875 to 0.21875
- value_bias: bfloat16 [768], P(('wide', 'narrow')), may hold values from -4 to 4
- output_weight: bfloat16 [768, 768], P(('wide', 'narrow')), may hold values from -0.625 to 0.625
- output_bias: bfloat16 [768], P(('wide', 'narrow')), may hold values from -4 to 4
- feed_gain: bfloat16 [768], P(('wide', 'narrow')), may hold values from 0.5 to 1.5
- feed_shift: bfloat16 [768], P(('wide', 'narrow')), may hold values from -4 to 4
- expand_weight: bfloat16 [768, 3072], P(('wide', 'narrow')), may hold values from -0.21875 to 0.21875
- expand_bias: bfloat16 [3072], P(('wide', 'narrow')), may hold values from -6 to 6
- reduce_weight: bfloat16 [3072, 768], P(('wide', 'narrow')), may hold values from -0.15625 to 0.15625
- reduce_bias: bfloat16 [768], P(('wide', 'narrow')), may hold values from -6 to 6
Outputs:
- layer_out: float32 [32768, 768], P(('wide', 'narrow'))
- tokens_grad: float32 [32768, 768], P(('wide', 'narrow'))
- attn_gain_grad: float32 [768], P(('wide', 'narrow'))
- attn_shift_grad: float32 [768], P(('wide', 'narrow'))
- dense_weight_grad: float32 [12, 768, 768], P(None, ('wide', 'narrow'))
- dense_bias_grad: float32 [9216], P(('wide', 'narrow'))
- logit_weight_grad: float32 [12, 768, 512], P(None, ('wide', 'narrow'))
- logit_bias_grad: float32 [6144], P(('wide', 'narrow'))
- value_weight_grad: float32 [768, 768], P(('wide', 'narrow'))
- value_bias_grad: float32 [768], P(('wide', 'narrow'))
- output_weight_grad: float32 [768, 768], P(('wide', 'narrow'))
- output_bias_grad: float32 [768], P(('wide', 'narrow'))
- feed_gain_grad: float32 [768], P(('wide', 'narrow'))
- feed_shift_grad: float32 [768], P(('wide', 'narrow'))
- expand_weight_grad: float32 [768, 3072], P(('wide', 'narrow'))
- expand_bias_grad: float32 [3072], P(('wide', 'narrow'))
- reduce_weight_grad: float32 [3072, 768], P(('wide', 'narrow'))
- reduce_bias_grad: float32 [768], P(('wide', 'narrow'))
Inputs may be any that keep to these rules, and one draw needn't show every extreme that they name: bucket_counts[d, k] is at most 2, 1 and 1 for k = 0, 1, 2; a device's live slots are its first ones in each bucket; in every draw one device has all its slots live and another has none.
All inputs are finite; a program needn't handle non-finite values.
Results may differ from a plain program's by a relative error of at most 0.012.
Values may be sent and summed in bfloat16 or wider, within the bound.
A program may use at most 384 MiB of HBM per device.

v0:
```python
import functools

import jax
import jax.numpy as jnp
import numpy as np
from jax import lax
from jax.experimental import pallas as pl
from jax.experimental.pallas import tpu as pltpu
from jax.sharding import PartitionSpec as P

D = 768
HEADS = 12
HEAD_DIM = 64
HIDDEN_SIZE = 768
L3 = 512
AXES = ("wide", "narrow")
L1 = 128
L2 = 256
S1 = 2
S2 = 1
S3 = 1

norm_eps = 1e-05
gelu_root = 0.7978845608028654
gelu_cube = 0.044715

MESH = pl.DeviceIdType.MESH
HBM = pl.BlockSpec(memory_space=pltpu.HBM)
VMEM = pl.BlockSpec(memory_space=pltpu.VMEM)
VMEM_LIMIT = 63 * 1024 * 1024
f32 = jnp.float32
bf16 = jnp.bfloat16

ROWS_DEV = 1024
CHIP_ROWS = 2048
HALF = 384
NN = (((1,), (0,)), ((), ()))
NT = (((1,), (1,)), ((), ()))
TN = (((0,), (0,)), ((), ()))


def dot(a, b, dims=NN):
    return lax.dot_general(a, b, dims, preferred_element_type=f32)


def gelu_both(v):
    sq = v * v
    t = jnp.tanh(v * (gelu_root + gelu_root * gelu_cube * sq))
    up = 0.5 + 0.5 * t
    slope = up + 0.5 * v * (1.0 - t * t) * (gelu_root + 3.0 * gelu_root * gelu_cube * sq)
    return v * up, slope


def norm_rows(x):
    mean = jnp.mean(x, axis=-1, keepdims=True)
    cen = x - mean
    inv = lax.rsqrt(jnp.mean(cen * cen, axis=-1, keepdims=True) + norm_eps)
    return cen * inv, inv


class Place:
    def __init__(self):
        w = lax.axis_index(AXES[0])
        n = lax.axis_index(AXES[1])
        self.w, self.n = w, n
        self.z, self.c = w // 2, w % 2
        self.nx = n + 1 - 2 * (n % 2)
        self.ny = (n + 2) % 4
        self.nd = 3 - n
        self.xdev = (w, self.nx)
        self.ydev = (w, self.ny)
        self.sib = (self.z * 2 + 1 - self.c, n)

    def zpos(self, i):
        return (self.z + i) % 4

    def zdev(self, zz):
        return (zz * 2 + self.c, self.n)

    def near(self):
        return [self.xdev, self.ydev, self.sib] + [self.zdev(self.zpos(i)) for i in (1, 2, 3)]


def greet(devs):
    bar = pltpu.get_barrier_semaphore()
    for dev in devs:
        pl.semaphore_signal(bar, inc=1, device_id=dev, device_id_type=MESH)
    pl.semaphore_wait(bar, len(devs))


def remote(src, dst, ssem, rsem, dev):
    return pltpu.make_async_remote_copy(
        src_ref=src, dst_ref=dst, send_sem=ssem, recv_sem=rsem, device_id=dev, device_id_type=MESH
    )


def k0_kernel(s_in, tok_in, dense, logit, vo, ff, s_all, tok, md, ml, mvo, mf, ss, sr, es, er):
    pc = Place()
    c = pc.c
    me = pc.w * 4 + pc.n
    bar = pltpu.get_barrier_semaphore()

    @pl.loop(1, 32)
    def _(j):
        t = (me + j) % 32
        pl.semaphore_signal(bar, inc=1, device_id=(t // 4, t % 4), device_id_type=MESH)

    pl.semaphore_wait(bar, 31)
    o = 1 - c

    @pl.loop(1, 32)
    def _(j):
        t = (me + j) % 32
        remote(s_in, s_all.at[me], ss.at[t], sr.at[me], (t // 4, t % 4)).start()

    pairs = [
        (dense.at[pl.ds(3 * o, 3)], md.at[:, c]),
        (logit.at[pl.ds(3 * o, 3)], ml.at[:, c]),
        (vo.at[o], mvo.at[c]),
        (ff.at[o], mf.at[:, c]),
        (tok_in, tok),
    ]
    rems = [remote(give, slot, es.at[i], er.at[i], pc.sib) for i, (give, slot) in enumerate(pairs)]
    for cp in rems:
        cp.start()
    s_all[me] = s_in[...]
    md[:, c] = dense[pl.ds(3 * c, 3)]
    ml[:, c] = logit[pl.ds(3 * c, 3)]
    mvo[c] = vo[c]
    mf[:, c] = ff[c]
    for cp in rems:
        cp.wait()

    @pl.loop(1, 32)
    def _(j):
        t = (me + j) % 32
        f = (me + 32 - j) % 32
        cp = remote(s_in, s_all.at[f], ss.at[t], sr.at[f], (t // 4, t % 4))
        cp.wait_send()
        cp.wait_recv()


def k0_call(s_in, tok, dense, logit, vo, ff):
    sds = jax.ShapeDtypeStruct
    return pl.pallas_call(
        k0_kernel,
        out_shape=(
            sds((32, 16, 128), bf16),
            sds((ROWS_DEV, D), bf16),
            sds((3, 2, 48, D), bf16),
            sds((3, 2, 48, L3), bf16),
            sds((2, 48, HALF), bf16),
            sds((2, 2, 48, D), bf16),
        ),
        in_specs=[VMEM, HBM, VMEM, VMEM, VMEM, VMEM],
        out_specs=(VMEM, HBM, VMEM, VMEM, VMEM, VMEM),
        scratch_shapes=[
            pltpu.SemaphoreType.DMA((32,)),
            pltpu.SemaphoreType.DMA((32,)),
            pltpu.SemaphoreType.DMA((5,)),
            pltpu.SemaphoreType.DMA((5,)),
        ],
        compiler_params=pltpu.CompilerParams(collective_id=0, has_side_effects=True),
        name="k0_exchange",
    )(s_in, tok, dense, logit, vo, ff)


class Gather:
    def __init__(self, pc, sems):
        self.pc = pc
        self.zs, self.zr, self.xs, self.xr, self.ys, self.yr, self.ds, self.dr, self.ls = sems

    def zcopy(self, k, src, buf, i, sender=None):
        pc = self.pc
        zz = pc.z if sender is None else sender
        return remote(src, buf.at[zz, :, pc.n], self.zs.at[k, i], self.zr.at[k, zz], pc.zdev(pc.zpos(i)))

    def zsend(self, k, src, buf):
        for i in (1, 2, 3):
            self.zcopy(k, src, buf, i).start()
        self.own(k, src, buf).start()

    def own(self, k, src, buf):
        return pltpu.make_async_copy(src, buf.at[self.pc.z, :, self.pc.n], self.ls.at[k])

    def xcopy(self, k, buf, zz, src=None, col=None):
        pc = self.pc
        col = pc.n if col is None else col
        slot = buf.at[zz, :, col]
        return remote(slot if src is None else src, slot, self.xs.at[k, zz], self.xr.at[k, zz], pc.xdev)

    def ycopy(self, k, buf, zz, src=None, col=None):
        pc = self.pc
        col = pc.n if col is None else col
        slot = buf.at[zz, :, col]
        return remote(slot if src is None else src, slot, self.ys.at[k, zz], self.yr.at[k, zz], pc.ydev)

    def col(self, k, src, buf, i):
        pc = self.pc
        zz = pc.zpos(i)
        if i:
            self.zcopy(k, src, buf, i, sender=zz).wait_recv()
        s = None if i else src
        self.xcopy(k, buf, zz, s).start()
        self.ycopy(k, buf, zz, s).start()

    def dcopy(self, k, buf, zz):
        pc = self.pc
        if zz < 2:
            slot, dev = buf.at[zz, :, pc.nx], pc.ydev
        else:
            slot, dev = buf.at[zz, :, pc.ny], pc.xdev
        return remote(slot, slot, self.ds.at[k, zz], self.dr.at[k, zz], dev)

    def diag(self, k, buf, zz):
        pc = self.pc
        self.xcopy(k, buf, zz, col=pc.nx).wait_recv()
        self.ycopy(k, buf, zz, col=pc.ny).wait_recv()
        self.dcopy(k, buf, zz).start()

    def fin(self, k, src, buf):
        for zz in range(4):
            remote(
                buf.at[zz, :, self.pc.nd],
                buf.at[zz, :, self.pc.nd],
                self.ds.at[k, zz],
                self.dr.at[k, zz],
                self.pc.xdev,
            ).wait_recv()
        self.own(k, src, buf).wait()

    def sent(self, k, src, buf):
        for i in (1, 2, 3):
            self.zcopy(k, src, buf, i).wait_send()
        for zz in range(4):
            self.xcopy(k, buf, zz).wait_send()
            self.ycopy(k, buf, zz).wait_send()
            self.dcopy(k, buf, zz).wait_send()


def gather_sems(k):
    dma = pltpu.SemaphoreType.DMA
    return [dma((k, 4))] * 8 + [dma((k,))]


def join_pair(stage, dst_of, rows_of):
    @pl.loop(0, 4)
    def _(zz):
        for cc in range(2):
            for nn in (0, 2):
                one = stage[zz, cc, nn].astype(f32)
                two = stage[zz, cc, nn + 1].astype(f32)
                row = pl.multiple_of(zz * 192 + cc * 96 + nn * 24, 16)
                for e in rows_of:
                    both = jnp.concatenate(
                        [one[24 * e : 24 * e + 24], two[24 * e : 24 * e + 24]], axis=0
                    )
                    dst_of(e, pl.ds(row, 48), both.astype(bf16))


def k1_kernel(
    tok, tok2, vec, db, lb, vb, mvo, md, ml, mf,
    ovo, gd, gl, ef, nrm_o, val_o, hid_o, slo_o, atl_o, atm_o, ats_o, wa_o, la_o, mix_o, vv_o,
    tokv, nrm, val, vst, vv, wst, lst, wv, lv, hidv, slov, atlv, atmv, atsv, mixv,
    zs, zr, xs, xr, ys, yr, ds, dr, ls, tsem, osem, wsem, lsem, ssem, rsem, msem,
):
    pc = Place()
    c = pc.c
    g = Gather(pc, (zs, zr, xs, xr, ys, yr, ds, dr, ls))
    tcopies = []
    for i, (ref, d) in enumerate(((tok, c), (tok2, 1 - c))):
        for j, (at, to) in enumerate(((512, d * 512), (0, 1024 + d * 512))):
            rows = pl.ds(pl.multiple_of(to, 512), 512)
            tcopies.append(pltpu.make_async_copy(ref.at[pl.ds(at, 512)], tokv.at[rows], tsem.at[2 * i + j]))
    for cp in tcopies:
        cp.start()
    greet(pc.near())

    vo_args = (0, mvo, ovo.at[c])
    dd = lambda p: (1 + 2 * p, md.at[p], gd.at[p])
    ll = lambda p: (2 + 2 * p, ml.at[p], gl.at[p])
    fa = (7, mf.at[0], ef.at[c, 0])
    fb = (8, mf.at[1], ef.at[c, 1])

    g.zsend(*vo_args)
    g.zsend(*dd(0))
    for i in range(4):
        g.col(*vo_args, i)
    g.zsend(*ll(0))
    for i in range(4):
        g.col(*dd(0), i)
    for zz in range(4):
        g.diag(vo_args[0], vo_args[2], zz)

    for cp in tcopies:
        cp.wait()

    @pl.loop(0, 8)
    def _(b):
        rows = pl.ds(pl.multiple_of(b * 256, 256), 256)
        unit, _ = norm_rows(tokv[rows].astype(f32))
        nrm[rows] = (unit * vec[0:1] + vec[1:2]).astype(bf16)

    nrm_copy = pltpu.make_async_copy(nrm, nrm_o, tsem.at[4])
    nrm_copy.start()
    g.zsend(*dd(1))
    for i in range(4):
        g.col(*ll(0), i)
    g.fin(*vo_args)
    vo_load = pltpu.make_async_copy(ovo.at[c], vst, tsem.at[5])
    vo_load.start()
    vo_swap = remote(ovo.at[c], ovo.at[c], ssem.at[0], rsem.at[0], pc.sib)
    vo_swap.start()
    vo_load.wait()

    def put_v(e, rows, x):
        vv[rows] = x

    join_pair(vst, put_v, (0,))

    @pl.loop(0, 4)
    def _(b):
        rows = pl.ds(pl.multiple_of(b * 512, 512), 512)
        val[rows] = (dot(nrm[rows], vv[...]) + vb[...]).astype(bf16)

    val_copy = pltpu.make_async_copy(val, val_o, tsem.at[6])
    val_copy.start()
    vv_copy = pltpu.make_async_copy(vv, vv_o, tsem.at[5])
    vv_copy.start()
    for zz in range(4):
        g.diag(dd(0)[0], dd(0)[2], zz)
    g.zsend(*ll(1))
    for i in range(2):
        g.col(*dd(1), i)
    for zz in range(4):
        g.diag(ll(0)[0], ll(0)[2], zz)
    g.fin(*dd(0))
    g.fin(*ll(0))

    lane = lax.broadcasted_iota(jnp.int32, (1, 128), 1)
    keeps = [(lane < HEAD_DIM).astype(bf16), (lane >= HEAD_DIM).astype(bf16)]

    def softmax(s):
        m = jnp.max(s, axis=-1, keepdims=True)
        ex = jnp.exp(s - m)
        return (ex / jnp.sum(ex, axis=-1, keepdims=True)).astype(bf16)

    @pl.loop(0, 3)
    def _(p):
        q = p + 1
        more = p < 2
        ka, kb = 1 + 2 * q, 2 + 2 * q

        def on_a(fn):
            @pl.when(more)
            def _():
                fn(ka, md.at[q % 3], gd.at[q % 3])

            @pl.when(jnp.logical_not(more))
            def _():
                fn(*fa)

        def on_b(fn):
            @pl.when(more)
            def _():
                fn(kb, ml.at[q % 3], gl.at[q % 3])

            @pl.when(jnp.logical_not(more))
            def _():
                fn(*fb)

        def on_next(fn):
            @pl.when(p == 0)
            def _():
                fn(5, md.at[2], gd.at[2])

            @pl.when(p == 1)
            def _():
                fn(*fa)

        def on_next_b(fn):
            @pl.when(p == 0)
            def _():
                fn(6, ml.at[2], gl.at[2])

            @pl.when(p == 1)
            def _():
                fn(*fb)

        def tick(pos):
            if pos == 0:
                on_a(lambda k, s, b: g.col(k, s, b, 2))
                on_a(lambda k, s, b: g.col(k, s, b, 3))
                on_next(g.zsend)
            elif pos == 1:
                on_b(lambda k, s, b: g.col(k, s, b, 0))
                on_b(lambda k, s, b: g.col(k, s, b, 1))
            elif pos == 2:
                on_a(lambda k, s, b: g.diag(k, b, 0))
                on_a(lambda k, s, b: g.diag(k, b, 2))
            elif pos == 3:
                on_b(lambda k, s, b: g.col(k, s, b, 2))
                on_b(lambda k, s, b: g.col(k, s, b, 3))
            elif pos == 4:
                on_a(lambda k, s, b: g.diag(k, b, 1))
                on_a(lambda k, s, b: g.diag(k, b, 3))
                on_next_b(g.zsend)
            elif pos == 5:
                on_next(lambda k, s, b: g.col(k, s, b, 0))
                on_b(lambda k, s, b: g.diag(k, b, 0))
            elif pos == 6:
                on_b(lambda k, s, b: g.diag(k, b, 2))
                on_next(lambda k, s, b: g.col(k, s, b, 1))
            elif pos == 7:
                on_b(lambda k, s, b: g.diag(k, b, 1))
                on_b(lambda k, s, b: g.diag(k, b, 3))

        wload = pltpu.make_async_copy(gd.at[p], wst, tsem.at[7])
        lload = pltpu.make_async_copy(gl.at[p], lst, tsem.at[8])
        wload.start()
        lload.start()
        wcopy = lambda r: pltpu.make_async_copy(wv, wa_o.at[pl.ds(2 * r, 2)], wsem)
        lcopy = lambda r: pltpu.make_async_copy(lv, la_o.at[pl.ds(2 * r, 2)], lsem)

        @pl.when(p > 0)
        def _():
            wcopy(p - 1).wait()
            lcopy(p - 1).wait()

        wload.wait()

        def put_w(e, rows, x):
            wv[e, rows] = x

        def put_l(e, rows, x):
            lv[e, rows] = x

        join_pair(wst, put_w, (0, 1))
        lload.wait()
        join_pair(lst, put_l, (0, 1))
        wcopy(p).start()
        lcopy(p).start()
        lanes = pl.ds(pl.multiple_of(p * 128, 128), 128)

        def out_copies(e, d, long, h):
            row = d * 512 if long else 1024 + d * 512
            rows = pl.ds(row, 512)
            cps = [
                pltpu.make_async_copy(hidv.at[e], hid_o.at[h, rows], osem.at[e, 0]),
                pltpu.make_async_copy(slov.at[e], slo_o.at[h, rows], osem.at[e, 1]),
            ]
            if long:
                cps.append(pltpu.make_async_copy(atlv.at[e], atl_o.at[h, pl.ds(d * 512, 512)], osem.at[e, 2]))
            else:
                part = pl.ds(d * 256, 256)
                cps.append(pltpu.make_async_copy(atmv.at[e], atm_o.at[h, part], osem.at[e, 3]))
                cps.append(pltpu.make_async_copy(atsv.at[e], ats_o.at[h, part], osem.at[e, 4]))
            return cps

        pos = 0
        for d in range(2):
            for long in (True, False):
                row = d * 512 if long else 1024 + d * 512
                rows = slice(row, row + 512)
                mixed = None
                for e in range(2):
                    h = 2 * p + e
                    pre = dot(nrm[rows], wv[e]) + db[pl.ds(h, 1)]
                    hid, slo = gelu_both(pre)
                    if d == 0 and long:

                        @pl.when(p > 0)
                        def _():
                            for cp in out_copies(e, 1, False, h):
                                cp.wait()
                    else:
                        for cp in out_copies(e, d if not long else d - 1, not long, h):
                            cp.wait()
                    hidv[e] = hid.astype(bf16)
                    slov[e] = slo.astype(bf16)
                    lbias = lb[pl.ds(h, 1)]
                    vpair = val[rows, lanes] * keeps[e]
                    if long:
                        att = softmax(dot(hidv[e], lv[e]) + lbias)
                        atlv[e] = att
                        m = dot(att, vpair)
                    else:
                        short = softmax(dot(hidv[e, 0:256], lv[e, :, 0:128]) + lbias[:, 0:128])
                        mid = softmax(dot(hidv[e, 256:512], lv[e, :, 0:256]) + lbias[:, 0:256])
                        atsv[e] = short
                        atmv[e] = mid
                        m = jnp.concatenate(
                            [
                                dot(short[0:128], vpair[0:128]),
                                dot(short[128:256], vpair[128:256]),
                                dot(mid, vpair[256:512]),
                            ],
                            axis=0,
                        )
                    mixed = m if mixed is None else mixed + m
                    for cp in out_copies(e, d, long, h):
                        cp.start()
                    tick(pos)
                    pos += 1
                mixv[rows, lanes] = mixed.astype(bf16)
        on_a(g.fin)
        on_b(g.fin)

        @pl.when(p == 2)
        def _():
            for e in range(2):
                for cp in out_copies(e, 1, False, 2 * p + e):
                    cp.wait()
            wcopy(p).wait()
            lcopy(p).wait()

    swaps = [remote(ef.at[c], ef.at[c], ssem.at[1], rsem.at[1], pc.sib), vo_swap]
    swaps[0].start()
    o = 1 - c
    for i, (start, to) in enumerate(((0, 512), (1024, 0))):
        mine = pltpu.make_async_copy(
            mixv.at[pl.ds(start + c * 512, 512)], mix_o.at[c, pl.ds(to, 512)], msem.at[i]
        )
        mine.start()
        other = remote(
            mixv.at[pl.ds(start + o * 512, 512)], mix_o.at[c, pl.ds(to, 512)], ssem.at[2 + i], rsem.at[2 + i], pc.sib
        )
        other.start()
        swaps += [mine, other]
    for cp in swaps + [nrm_copy, val_copy, vv_copy]:
        cp.wait()
    g.sent(*vo_args)
    for p in range(3):
        g.sent(*dd(p))
        g.sent(*ll(p))
    g.sent(*fa)
    g.sent(*fb)


def k1_call(tok, tok2, vec, db, lb, vb, mvo, md, ml, mf):
    sds = jax.ShapeDtypeStruct
    dma = pltpu.SemaphoreType.DMA
    return pl.pallas_call(
        k1_kernel,
        out_shape=(
            sds((2, 4, 2, 4, 48, HALF), bf16),
            sds((3, 4, 2, 4, 48, D), bf16),
            sds((3, 4, 2, 4, 48, L3), bf16),
            sds((2, 2, 4, 2, 4, 48, D), bf16),
            sds((CHIP_ROWS, D), bf16),
            sds((CHIP_ROWS, HALF), bf16),
            sds((6, CHIP_ROWS, HIDDEN_SIZE), bf16),
            sds((6, CHIP_ROWS, HIDDEN_SIZE), bf16),
            sds((6, 1024, L3), bf16),
            sds((6, 512, L2), bf16),
            sds((6, 512, L1), bf16),
            sds((6, D, HIDDEN_SIZE), bf16),
            sds((6, HIDDEN_SIZE, L3), bf16),
            sds((2, ROWS_DEV, HALF), bf16),
            sds((D, HALF), bf16),
        ),
        in_specs=[HBM] * 2 + [VMEM] * 8,
        out_specs=(HBM,) * 15,
        scratch_shapes=[
            pltpu.VMEM((CHIP_ROWS, D), bf16),
            pltpu.VMEM((CHIP_ROWS, D), bf16),
            pltpu.VMEM((CHIP_ROWS, HALF), bf16),
            pltpu.VMEM((4, 2, 4, 48, HALF), bf16),
            pltpu.VMEM((D, HALF), bf16),
            pltpu.VMEM((4, 2, 4, 48, D), bf16),
            pltpu.VMEM((4, 2, 4, 48, L3), bf16),
            pltpu.VMEM((2, D, HIDDEN_SIZE), bf16),
            pltpu.VMEM((2, HIDDEN_SIZE, L3), bf16),
            pltpu.VMEM((2, 512, HIDDEN_SIZE), bf16),
            pltpu.VMEM((2, 512, HIDDEN_SIZE), bf16),
            pltpu.VMEM((2, 512, L3), bf16),
            pltpu.VMEM((2, 256, L2), bf16),
            pltpu.VMEM((2, 256, L1), bf16),
            pltpu.VMEM((CHIP_ROWS, HALF), bf16),
        ]
        + gather_sems(9)
        + [dma((9,)), dma((2, 5)), dma, dma, dma((4,)), dma((4,)), dma((2,))],
        compiler_params=pltpu.CompilerParams(
            collective_id=1, has_side_effects=True, vmem_limit_bytes=VMEM_LIMIT
        ),
        name="k1_attention",
    )(tok, tok2, vec, db, lb, vb, mvo, md, ml, mf)


def prepare(tokens, attn_gain, attn_shift, dense_weight, dense_bias, logit_weight, logit_bias, value_weight,
            value_bias, output_weight, output_bias, feed_gain, feed_shift, expand_weight, expand_bias,
            reduce_weight, reduce_bias):
    core = lax.axis_index(AXES[0]) % 2
    small = jnp.concatenate(
        [attn_gain, attn_shift, value_bias, output_bias, feed_gain, feed_shift, reduce_bias,
         expand_bias, logit_bias, dense_bias, jnp.zeros((2048 - 744,), bf16)]
    ).reshape(16, 128)
    dense = dense_weight.reshape(6, 48, D)
    logit = logit_weight.reshape(6, 48, L3)
    vo = jnp.stack([value_weight.reshape(24, 2, HALF), output_weight.reshape(24, 2, HALF)]).transpose(2, 0, 1, 3)
    vo = vo.reshape(2, 48, HALF)
    ff = jnp.stack(
        [expand_weight.reshape(24, 4, D).transpose(1, 0, 2).reshape(2, 48, D), reduce_weight.reshape(2, 48, D)]
    )
    s_all, tok2, md, ml, mvo, mf = k0_call(small, tokens, dense, logit, vo, ff)
    flat = s_all.reshape(32, 2048)[:, :744].astype(f32)
    vec = flat[:, :168].reshape(32, 7, 24).transpose(1, 0, 2).reshape(7, D)
    eb = flat[:, 168:264].reshape(4, D)
    lb = lax.dynamic_slice(flat[:, 264:456].reshape(HEADS, L3), (6 * core, 0), (6, L3))
    db = lax.dynamic_slice(flat[:, 456:744].reshape(HEADS, HIDDEN_SIZE), (6 * core, 0), (6, HIDDEN_SIZE))
    vb = lax.dynamic_slice(vec[2:3], (0, HALF * core), (1, HALF))
    return tok2, vec, eb, lb, db, vb, md, ml, mvo, mf


def k2_kernel(
    x, cot, counts, mix, ovo, ef, vec, eb,
    lay_o, gres_o, gmix_o, def_o, do_o, sums_o,
    ev, rv, ow, inner, ge, n2, gf, ga, acc, dst, rsem, dsem, osem,
):
    oloads = []
    for half in range(2):
        lanes = pl.ds(half * HALF, HALF)
        oloads.append(pltpu.make_async_copy(ovo.at[half], dst.at[0, :, :, :, :, lanes], osem.at[half]))
    loads = [pltpu.make_async_copy(ef.at[0, f], dst.at[1 - f], dsem.at[1 - f]) for f in range(2)]
    for cp in oloads:
        cp.start()
    loads[0].start()
    rloads = []
    for f in range(2):
        for j in range(4):
            rloads.append(
                pltpu.make_async_copy(ef.at[1, f, j], rv.at[j, :, :, pl.ds(48 * f, 48)], rsem.at[f, j])
            )
    for cp in rloads:
        cp.start()

    def put_o(e, rows, v):
        ow[rows] = v

    for cp in oloads:
        cp.wait()
    join_pair(dst.at[0], put_o, (1,))
    loads[1].start()
    for f in range(2):

        def put_e(e, rows, v):
            ev[2 * f + e, rows] = v

        loads[f].wait()
        join_pair(dst.at[1 - f], put_e, (0, 1))
    for cp in rloads:
        cp.wait()
    fg, fs = vec[4:5], vec[5:6]
    sums_o[...] = jnp.zeros_like(sums_o)

    @pl.loop(0, 4)
    def _(b):
        rows = pl.ds(pl.multiple_of(b * 256, 256), 256)
        mixed = jnp.concatenate([mix[0, rows], mix[1, rows]], axis=1)
        res = x[rows].astype(f32) + (dot(mixed, ow[...]) + vec[3:4])
        unit, inv = norm_rows(res)
        n2v = (unit * fg + fs).astype(bf16)
        n2[rows] = n2v
        later = jnp.where(b == 1, counts[0, 1], counts[0, 2])
        low = jnp.where(b == 0, counts[0, 0], later) >= 1
        high = jnp.where(b == 0, counts[0, 0] - 1, later) >= 1
        top = lax.broadcasted_iota(jnp.int32, (256, 1), 0) < L1
        alive = jnp.where(top, jnp.where(low, 1.0, 0.0), jnp.where(high, 1.0, 0.0))
        gout = cot[rows].astype(f32) * alive
        gfb = gout.astype(bf16)
        gf[rows] = gfb
        feed = None
        gn2 = None
        for j in range(4):
            cols = slice(j * D, j * D + D)
            rj = rv[j].reshape(D, D)
            hid, slo = gelu_both(dot(n2v, ev[j]) + eb[j : j + 1])
            hb = hid.astype(bf16)
            inner[rows, cols] = hb
            f_j = dot(hb, rj)
            feed = f_j if feed is None else feed + f_j
            geb = (dot(gfb, rj, NT) * slo).astype(bf16)
            ge[rows, cols] = geb
            g_j = dot(geb, ev[j], NT)
            gn2 = g_j if gn2 is None else gn2 + g_j
        lay_o[rows] = alive * (res + (feed + vec[6:7]))
        q = gn2 * fg
        gres = gout + inv * (
            q - jnp.mean(q, axis=-1, keepdims=True) - unit * jnp.mean(q * unit, axis=-1, keepdims=True)
        )
        gres_o[rows] = gres
        gab = gres.astype(bf16)
        ga[rows] = gab
        gm = dot(gab, ow[...], NT).astype(bf16)
        gmix_o[0, rows] = gm[:, :HALF]
        gmix_o[1, rows] = gm[:, HALF:]
        sums_o[0:1] += jnp.sum(gn2 * unit, axis=0, keepdims=True)
        sums_o[1:2] += jnp.sum(gn2, axis=0, keepdims=True)

    ones = jnp.ones((8, ROWS_DEV), bf16)
    sums_o[2:3] = dot(ones, gf[...])[0:1]
    sums_o[3:4] = dot(ones, ga[...])[0:1]

    def out_copy(t, f):
        return pltpu.make_async_copy(dst.at[f], def_o.at[t, f], dsem.at[f])

    for f in range(2):
        for e in range(2):
            j = 2 * f + e
            sums_o[4 + j : 5 + j] = dot(ones, ge[:, j * D : j * D + D])[0:1]
            acc[e] = dot(n2[...], ge[:, j * D : j * D + D], TN)

        @pl.loop(0, 4)
        def _(zz):
            for i in range(8):
                row = pl.ds(pl.multiple_of(zz * 192 + i * 24, 8), 24)
                both = jnp.concatenate([acc[0, row], acc[1, row]], axis=0)
                dst[f, zz, i // 4, i % 4] = both.astype(bf16)

        out_copy(0, f).start()
    for j in range(4):
        acc[j % 2] = dot(inner[:, j * D : j * D + D], gf[...], TN)
        if j == 0:
            out_copy(0, 0).wait()
            out_copy(0, 1).wait()
        for i in range(8):
            for f in range(2):
                at = i * 96 + f * 48
                dst[f, j, i // 4, i % 4] = acc[j % 2, at : at + 48].astype(bf16)
    for f in range(2):
        out_copy(1, f).start()
    zero = jnp.zeros((24, HALF), f32)
    for hh in range(2):
        acc[0, 0:HALF] = dot(mix[hh], ga[...], TN)
        for i in range(16):
            for half in range(2):
                part = acc[0, i * 24 : i * 24 + 24, half * HALF : half * HALF + HALF]
                do_o[half, 2 * hh + i // 8, (i // 4) % 2, i % 4] = jnp.concatenate([zero, part], axis=0).astype(bf16)
    for f in range(2):
        out_copy(1, f).wait()


def k2_call(x, cot, counts, mix, ovo, ef, vec, eb):
    sds = jax.ShapeDtypeStruct
    dma = pltpu.SemaphoreType.DMA
    return pl.pallas_call(
        k2_kernel,
        out_shape=(
            sds((ROWS_DEV, D), f32),
            sds((ROWS_DEV, D), f32),
            sds((2, ROWS_DEV, HALF), bf16),
            sds((2, 2, 4, 2, 4, 48, D), bf16),
            sds((2, 4, 2, 4, 48, HALF), bf16),
            sds((8, D), f32),
        ),
        in_specs=[VMEM, VMEM, pl.BlockSpec(memory_space=pltpu.SMEM), VMEM] + [HBM] * 2 + [VMEM] * 2,
        out_specs=(VMEM, VMEM, VMEM, HBM, VMEM, VMEM),
        scratch_shapes=[
            pltpu.VMEM((4, D, D), bf16),
            pltpu.VMEM((4, 2, 4, 96, D), bf16),
            pltpu.VMEM((D, D), bf16),
            pltpu.VMEM((ROWS_DEV, 4 * D), bf16),
            pltpu.VMEM((ROWS_DEV, 4 * D), bf16),
            pltpu.VMEM((ROWS_DEV, D), bf16),
            pltpu.VMEM((ROWS_DEV, D), bf16),
            pltpu.VMEM((ROWS_DEV, D), bf16),
            pltpu.VMEM((2, D, D), f32),
            pltpu.VMEM((2, 4, 2, 4, 48, D), bf16),
            dma((2, 4)),
            dma((2,)),
            dma((2,)),
        ],
        compiler_params=pltpu.CompilerParams(vmem_limit_bytes=VMEM_LIMIT),
        name="k2_feed",
    )(x, cot, counts, mix, ovo, ef, vec, eb)


class Scatter:
    def __init__(self, pc, sems):
        self.pc = pc
        self.as_, self.ar, self.xs, self.xr, self.ys, self.yr, self.zs, self.zr, self.os, self.or_ = sems

    def acopy(self, k, p5, bufs, zz):
        dev = self.pc.xdev if zz < 2 else self.pc.ydev
        return remote(p5.at[zz, :, self.pc.nd], bufs[0].at[zz], self.as_.at[k, zz], self.ar.at[k, zz], dev)

    def xcopy(self, k, p5, bufs, zz):
        return remote(p5.at[zz, :, self.pc.nx], bufs[1].at[zz], self.xs.at[k, zz], self.xr.at[k, zz], self.pc.xdev)

    def ycopy(self, k, p5, bufs, zz):
        return remote(p5.at[zz, :, self.pc.ny], bufs[2].at[zz], self.ys.at[k, zz], self.yr.at[k, zz], self.pc.ydev)

    def zcopy(self, k, p5, bufs, i):
        zz = self.pc.zpos(i)
        return remote(
            p5.at[zz, :, self.pc.n], bufs[3].at[i - 1], self.zs.at[k, i], self.zr.at[k, i], self.pc.zdev(zz)
        )

    def one(self, k, p5, bufs):
        for zz in range(4):
            self.acopy(k, p5, bufs, zz).start()
        for zz in range(4):
            (self.xcopy if zz < 2 else self.ycopy)(k, p5, bufs, zz).start()

    def two(self, k, p5, bufs, zz):
        col = self.pc.ny if zz < 2 else self.pc.nx
        self.acopy(k, p5, bufs, zz).wait_recv()
        p5[zz, :, col] = (p5[zz, :, col].astype(f32) + bufs[0][zz].astype(f32)).astype(bf16)
        (self.ycopy if zz < 2 else self.xcopy)(k, p5, bufs, zz).start()

    def column(self, k, p5, bufs, zz):
        self.xcopy(k, p5, bufs, zz).wait_recv()
        self.ycopy(k, p5, bufs, zz).wait_recv()
        return p5[zz, :, self.pc.n].astype(f32) + bufs[1][zz].astype(f32) + bufs[2][zz].astype(f32)

    def three(self, k, p5, bufs, i):
        zz = self.pc.zpos(i)
        p5[zz, :, self.pc.n] = self.column(k, p5, bufs, zz).astype(bf16)
        self.zcopy(k, p5, bufs, i).start()

    def outs(self, k, st, out):
        c = self.pc.c
        return (
            pltpu.make_async_copy(st.at[c], out, self.os.at[k, 1]),
            remote(st.at[1 - c], out, self.os.at[k, 0], self.or_.at[k], self.pc.sib),
        )

    def four(self, k, p5, bufs, st, out):
        total = self.column(k, p5, bufs, self.pc.z)
        for i in (1, 2, 3):
            self.zcopy(k, p5, bufs, i).wait_recv()
            total = total + bufs[3][i - 1].astype(f32)
        st[...] = total
        for cp in self.outs(k, st, out):
            cp.start()

    def sent(self, k, p5, bufs):
        for zz in range(4):
            self.acopy(k, p5, bufs, zz).wait_send()
            self.xcopy(k, p5, bufs, zz).wait_send()
            self.ycopy(k, p5, bufs, zz).wait_send()
        for i in (1, 2, 3):
            self.zcopy(k, p5, bufs, i).wait_send()


def k3_kernel(
    def_in, do_in, nrm_i, val_i, gmix, hid_i, slo_i, atl_i, atm_i, ats_i, wa_i, la_i, vv_i, tok, gres, vec,
    tg_o, od, ol, ofe, ovo, db_o, lb_o, vb_o, ag_o,
    nrm, val, gm, gn, hid, slo, atl, atm, ats, gsl, gsm, gd, wv, lv, dwf, vsb, vv, own,
    pd, pll, pv, ad, xd, yd, zd, al, xl, yl, zl, av, xv, yv, zv, std, stl, stv,
    as_, ar, xs, xr, ys, yr, zs, zr, os_, or_, lsem, ssem, rsem, gs_, gr_, free, hsem, fsem, dsem,
):
    pc = Place()
    c = pc.c
    o = 1 - c
    s = Scatter(pc, (as_, ar, xs, xr, ys, yr, zs, zr, os_, or_))
    copy = pltpu.make_async_copy
    first = [copy(nrm_i, nrm, lsem.at[0]), copy(val_i, val, lsem.at[1]), copy(vv_i, vv, lsem.at[2])]
    for i, (at, to) in enumerate(((512, 0), (0, 1024))):
        first.append(copy(gmix.at[c, pl.ds(at, 512)], gm.at[pl.ds(pl.multiple_of(to + c * 512, 512), 512)], lsem.at[4 + i]))
    for cp in first:
        cp.start()

    def att_loads(h):
        return [copy(atl_i.at[h], atl, hsem.at[0]), copy(atm_i.at[h], atm, hsem.at[1]), copy(ats_i.at[h], ats, hsem.at[2])]

    hid_load = lambda h: copy(hid_i.at[h], hid, hsem.at[3])
    w_load = lambda h: copy(wa_i.at[h], wv, hsem.at[4])
    l_load = lambda h: copy(la_i.at[h], lv, hsem.at[5])
    slo_load = lambda h, b: copy(slo_i.at[h, pl.ds(b * 512, 512)], slo.at[b % 2], hsem.at[6 + b % 2])
    for cp in att_loads(0) + [hid_load(0), l_load(0), slo_load(0, 0), slo_load(0, 1), w_load(0)]:
        cp.start()
    own_load = lambda f, zz: copy(def_in.at[c, f, zz], own.at[zz % 2], fsem.at[zz % 2])
    own_load(0, 0).start()
    own_load(0, 1).start()

    greet(pc.near())
    swaps = []
    for f in range(2):
        swaps.append(remote(def_in.at[o, f], pd.at[f], ssem.at[f], rsem.at[f], pc.sib))
    swaps.append(remote(do_in.at[o], pv, ssem.at[2], rsem.at[2], pc.sib))
    for i, (at, to) in enumerate(((512, 0), (0, 1024))):
        swaps.append(
            remote(
                gmix.at[o, pl.ds(at, 512)],
                gm.at[pl.ds(pl.multiple_of(to + c * 512, 512), 512)],
                ssem.at[3 + i],
                rsem.at[3 + i],
                pc.sib,
            )
        )
    for i in (3, 4, 0, 1, 2):
        swaps[i].start()

    def d_args(k):
        slot = k % 3
        return pd.at[slot], (ad.at[k], xd.at[k], yd.at[k], zd.at[k])

    def l_args(p):
        return pll.at[p % 2], (al.at[p], xl.at[p], yl.at[p], zl.at[p])

    v_args = (pv, (av, xv, yv, zv))
    gn[...] = jnp.zeros_like(gn)
    gsm[...] = jnp.zeros_like(gsm)

    for f in range(2):
        swaps[f].wait()
        for zz in range(4):
            own_load(f, zz).wait()
            pd[f, zz] = (pd[f, zz].astype(f32) + own[zz % 2].astype(f32)).astype(bf16)
            if zz < 2:
                own_load(f, zz + 2).start()
            elif f == 0:
                own_load(1, zz - 2).start()
        s.one(f, *d_args(f))
    dloads = []
    for zz in range(4):
        lanes = pl.ds(HALF * (zz % 2), HALF)
        dloads.append(copy(do_in.at[c, zz], own.at[zz // 2, :, :, :, lanes], dsem.at[zz]))
    for cp in dloads:
        cp.start()
    swaps[3].wait()
    swaps[4].wait()
    for cp in first:
        cp.wait()

    lane = lax.broadcasted_iota(jnp.int32, (1, 128), 1)
    keeps = [(lane < HEAD_DIM).astype(bf16), (lane >= HEAD_DIM).astype(bf16)]
    ones = jnp.ones((8, 1024), bf16)

    def score_grad(att, g):
        a = att.astype(f32)
        t = a * g
        return (t - a * jnp.sum(t, axis=-1, keepdims=True)).astype(bf16)

    def put_pair(p5, half, e, width):
        @pl.loop(0, 2)
        def _(zi):
            for i in range(8):
                row = pl.ds(pl.multiple_of(zi * 192 + i * 24, 8), 24)
                part = dwf[row, 0:width]
                if e == 0:
                    both = jnp.concatenate([part, part], axis=0)
                else:
                    old = p5[2 * half + zi, i // 4, i % 4].astype(f32)
                    both = jnp.concatenate([old[0:24], part], axis=0)
                p5[2 * half + zi, i // 4, i % 4] = both.astype(bf16)

    @pl.loop(0, 3)
    def _(p):
        lanes = pl.ds(pl.multiple_of(p * 128, 128), 128)
        begin = p == 0
        later = p > 0
        kd = p + 2
        dslot = kd % 3

        def on_a(fn):
            @pl.when(begin)
            def _():
                fn(0, *d_args(0))

            @pl.when(later)
            def _():
                fn(kd - 1, *d_args(kd - 1))

        def on_b(fn):
            @pl.when(begin)
            def _():
                fn(1, *d_args(1))

            @pl.when(later)
            def _():
                fn(5 + (p + 2) % 3, *l_args((p + 2) % 3))

        def four_a():
            @pl.when(begin)
            def _():
                s.four(0, *d_args(0), std.at[0], ofe.at[c, 0])

            @pl.when(p == 2)
            def _():
                for cp in s.outs(0, std.at[0], ofe.at[c, 0]):
                    cp.wait()

            @pl.when(later)
            def _():
                s.four(kd - 1, *d_args(kd - 1), std.at[(kd - 1) % 3], od.at[3 * c + (p + 2) % 3])

        def four_b():
            @pl.when(begin)
            def _():
                s.four(1, *d_args(1), std.at[1], ofe.at[c, 1])

            @pl.when(later)
            def _():
                r = (p + 2) % 3
                s.four(5 + r, *l_args(r), stl.at[r], ol.at[3 * c + r])

        for e in range(2):
            h = 2 * p + e
            more = h < 5

            def ahead(*cps):
                @pl.when(more)
                def _():
                    for cp in cps:
                        cp.start()

            for cp in att_loads(h):
                cp.wait()
            for b in range(4):
                at = b * 512
                rows = slice(at, at + 512)
                gpair = gm[rows, lanes]
                vpair = val[rows, lanes] * keeps[e]
                gkeep = gpair * keeps[e]
                if b < 2:
                    att = atl[rows]
                    gsl[rows] = score_grad(att, dot(gpair, vpair, NT))
                    vs = dot(att, gkeep, TN)
                else:
                    part = slice((b - 2) * 256, (b - 2) * 256 + 256)
                    sh, mi = ats[part], atm[part]
                    g_sh = jnp.concatenate(
                        [dot(gpair[0:128], vpair[0:128], NT), dot(gpair[128:256], vpair[128:256], NT)], axis=0
                    )
                    at2 = (b - 2) * 512
                    gsm[at2 : at2 + 256, 0:128] = score_grad(sh, g_sh)
                    gsm[at2 + 256 : at2 + 512] = score_grad(mi, dot(gpair[256:512], vpair[256:512], NT))
                    vs = jnp.concatenate(
                        [
                            dot(sh[0:128], gkeep[0:128], TN),
                            dot(sh[128:256], gkeep[128:256], TN),
                            dot(mi, gkeep[256:512], TN),
                        ],
                        axis=0,
                    )
                if e == 0:
                    vsb[rows] = vs.astype(bf16)
                else:
                    gm[rows, lanes] = vsb[rows] + vs.astype(bf16)
            ahead(*att_loads(h + 1))
            lsum = dot(ones, gsl[...])
            lb_o[pl.ds(h, 1)] = lsum[0:1]
            lb_o[pl.ds(h, 1), 0:256] += dot(ones, gsm[...])[0:1]
            if e == 0:
                on_a(lambda k, p5, bufs: s.two(k, p5, bufs, 0))
                on_a(lambda k, p5, bufs: s.two(k, p5, bufs, 2))
            else:
                for i in (1, 2, 3):
                    on_a(lambda k, p5, bufs, i=i: s.three(k, p5, bufs, i))
            if e == 0:

                @pl.when(p == 2)
                def _():
                    s.sent(5, *l_args(0))

            hid_load(h).wait()
            for half in range(2):
                cols = slice(half * HALF, half * HALF + HALF)
                dwf[:, 0:512] = dot(hid[0:1024, cols], gsl[...], TN)
                dwf[:, 0:256] += dot(hid[1024:2048, cols], gsm[...], TN)
                put_pair(pll.at[p % 2], half, e, 512)
            ahead(hid_load(h + 1))
            if e == 1:
                s.one(5 + p, *l_args(p))
            else:
                on_a(lambda k, p5, bufs: s.two(k, p5, bufs, 1))
                on_a(lambda k, p5, bufs: s.two(k, p5, bufs, 3))
            l_load(h).wait()
            for b in range(4):
                rows = slice(b * 512, b * 512 + 512)
                slo_load(h, b).wait()
                if b < 2:
                    gh = dot(gsl[rows], lv[...], NT)
                else:
                    gh = dot(gsm[(b - 2) * 512 : (b - 2) * 512 + 512], lv[:, 0:256], NT)
                gd[rows] = (gh * slo[b % 2].astype(f32)).astype(bf16)
                if b < 2:
                    slo_load(h, b + 2).start()
                else:
                    ahead(slo_load(h + 1, b - 2))
            ahead(l_load(h + 1))
            db_o[pl.ds(h, 1)] = (dot(ones, gd[0:1024]) + dot(ones, gd[1024:2048]))[0:1]
            if e == 0:
                on_b(lambda k, p5, bufs: s.two(k, p5, bufs, 0))
                on_b(lambda k, p5, bufs: s.two(k, p5, bufs, 2))
            else:
                for i in (1, 2, 3):
                    on_b(lambda k, p5, bufs, i=i: s.three(k, p5, bufs, i))
            if e == 0:

                @pl.when(later)
                def _():
                    s.sent(kd - 3, *d_args(kd - 3))

            for half in range(2):
                cols = slice(half * HALF, half * HALF + HALF)
                dwf[...] = dot(nrm[:, cols], gd[...], TN)
                put_pair(pd.at[dslot], half, e, D)
            if e == 1:
                s.one(kd, *d_args(kd))
                four_a()
            else:
                on_b(lambda k, p5, bufs: s.two(k, p5, bufs, 1))
                on_b(lambda k, p5, bufs: s.two(k, p5, bufs, 3))
            w_load(h).wait()

            @pl.loop(0, 4)
            def _(b):
                rows = pl.ds(pl.multiple_of(b * 512, 512), 512)
                gn[rows] += dot(gd[rows], wv[...], NT)

            ahead(w_load(h + 1))
            if e == 1:
                four_b()

    vb_o[...] = dot(ones, gm[0:1024]) + dot(ones, gm[1024:2048])
    swaps[2].wait()
    for cp in dloads:
        cp.wait()
    for half in range(2):
        cols = slice(half * HALF, half * HALF + HALF)
        dwf[:, 0:HALF] = dot(nrm[:, cols], gm[...], TN)

        for zi in range(2):

            @pl.loop(0, 8)
            def _(i):
                row = pl.ds(pl.multiple_of(zi * 192 + i * 24, 8), 24)
                part = dwf[row, 0:HALF]
                at = (2 * half + zi, i // 4, i % 4)
                mine = own[half, i // 4, i % 4, :, HALF * zi : HALF * zi + HALF]
                both = pv[at].astype(f32) + mine.astype(f32)
                pv[at] = jnp.concatenate([part, both[24:48]], axis=0).astype(bf16)

    s.one(8, *v_args)
    for zz in (0, 2):
        s.two(4, *d_args(4), zz)
    for zz in (0, 2):
        s.two(7, *l_args(2), zz)
    pl.semaphore_signal(free, inc=1, device_id=pc.sib, device_id_type=MESH)

    @pl.loop(0, 4)
    def _(b):
        rows = pl.ds(pl.multiple_of(b * 512, 512), 512)
        gn[rows] += dot(gm[rows], vv[...], NT)

    for zz in (1, 3):
        s.two(4, *d_args(4), zz)
    for zz in (1, 3):
        s.two(7, *l_args(2), zz)
    for zz in (0, 2, 1, 3):
        s.two(8, *v_args, zz)
    other = lambda to: pl.ds(pl.multiple_of(to + o * 512, 512), 512)
    mine = lambda to: pl.ds(pl.multiple_of(to + c * 512, 512), 512)
    hid[0:512] = gn[other(1024)].astype(bf16)
    hid[512:1024] = gn[other(0)].astype(bf16)
    pl.semaphore_wait(free, 1)
    gswap = remote(hid.at[pl.ds(0, 1024)], gd.at[pl.ds(0, 1024)], gs_, gr_, pc.sib)
    gswap.start()
    tloads = [copy(tok.at[pl.ds(i * 512, 512)], slo.at[i], hsem.at[6 + i]) for i in range(2)]
    for cp in tloads:
        cp.start()
    for i in (1, 2, 3):
        s.three(4, *d_args(4), i)
    for i in (1, 2, 3):
        s.three(7, *l_args(2), i)
    for cp in tloads:
        cp.wait()
    gswap.wait()
    ag_o[...] = jnp.zeros_like(ag_o)

    @pl.loop(0, 4)
    def _(b):
        nat = pl.ds(pl.multiple_of(b * 256, 256), 256)
        trow = pl.ds(pl.multiple_of(jnp.where(b < 2, 1024 + b * 256, b * 256 - 512) + c * 512, 256), 256)
        load = copy(gres.at[nat], dwf.at[pl.ds(0, 256)], lsem.at[6])
        load.start()
        unit, inv = norm_rows(slo[b // 2, pl.ds(pl.multiple_of((b % 2) * 256, 256), 256)].astype(f32))
        g = gn[trow] + gd[nat].astype(f32)
        q = g * vec[0:1]
        back = inv * (q - jnp.mean(q, axis=-1, keepdims=True) - unit * jnp.mean(q * unit, axis=-1, keepdims=True))
        load.wait()
        dwf[0:256] = dwf[0:256] + back
        ag_o[0:1] += jnp.sum(g * unit, axis=0, keepdims=True)
        ag_o[1:2] += jnp.sum(g, axis=0, keepdims=True)
        store = copy(dwf.at[pl.ds(0, 256)], tg_o.at[nat], lsem.at[7])
        store.start()
        store.wait()

    for i in (1, 2, 3):
        s.three(8, *v_args, i)
    for cp in s.outs(1, std.at[1], ofe.at[c, 1]):
        cp.wait()
    s.four(4, *d_args(4), std.at[1], od.at[3 * c + 2])
    s.four(7, *l_args(2), stl.at[2], ol.at[3 * c + 2])
    s.four(8, *v_args, stv, ovo.at[c])
    ends = []
    for p in range(3):
        ends.append(s.outs(2 + p, std.at[(2 + p) % 3], od.at[3 * c + p]))
        ends.append(s.outs(5 + p, stl.at[p], ol.at[3 * c + p]))
    ends.append(s.outs(8, stv, ovo.at[c]))
    for pair in ends:
        for cp in pair:
            cp.wait()
    for k in (2, 3, 4):
        s.sent(k, *d_args(k))
    for p in (1, 2):
        s.sent(5 + p, *l_args(p))
    s.sent(8, *v_args)


def k3_call(*args):
    sds = jax.ShapeDtypeStruct
    dma = pltpu.SemaphoreType.DMA
    V = pltpu.VMEM

    def bufs(shape, width):
        return [V(shape + (4, 2, 48, width), bf16)] * 3 + [V(shape + (3, 2, 48, width), bf16)]

    return pl.pallas_call(
        k3_kernel,
        out_shape=(
            sds((ROWS_DEV, D), f32),
            sds((6, 48, D), f32),
            sds((6, 48, L3), f32),
            sds((2, 2, 48, D), f32),
            sds((2, 48, HALF), f32),
            sds((8, D), f32),
            sds((8, L3), f32),
            sds((8, HALF), f32),
            sds((8, D), f32),
        ),
        in_specs=[HBM] * 15 + [VMEM],
        out_specs=(HBM,) * 5 + (VMEM,) * 4,
        scratch_shapes=[
            V((CHIP_ROWS, D), bf16),
            V((CHIP_ROWS, HALF), bf16),
            V((CHIP_ROWS, HALF), bf16),
            V((CHIP_ROWS, D), f32),
            V((CHIP_ROWS, HIDDEN_SIZE), bf16),
            V((2, 512, HIDDEN_SIZE), bf16),
            V((1024, L3), bf16),
            V((512, L2), bf16),
            V((512, L1), bf16),
            V((1024, L3), bf16),
            V((1024, L2), bf16),
            V((CHIP_ROWS, HIDDEN_SIZE), bf16),
            V((D, HIDDEN_SIZE), bf16),
            V((HIDDEN_SIZE, L3), bf16),
            V((HALF, D), f32),
            V((CHIP_ROWS, 128), bf16),
            V((D, HALF), bf16),
            V((2, 2, 4, 48, D), bf16),
            V((3, 4, 2, 4, 48, D), bf16),
            V((2, 4, 2, 4, 48, L3), bf16),
            V((4, 2, 4, 48, HALF), bf16),
        ]
        + bufs((5,), D)
        + bufs((3,), L3)
        + bufs((), HALF)
        + [V((3, 2, 48, D), f32), V((3, 2, 48, L3), f32), V((2, 48, HALF), f32)]
        + [dma((9, 4))] * 8
        + [dma((9, 2)), dma((9,)), dma((8,)), dma((5,)), dma((5,)), dma, dma, pltpu.SemaphoreType.REGULAR]
        + [dma((8,)), dma((2,)), dma((4,))],
        compiler_params=pltpu.CompilerParams(
            collective_id=2, has_side_effects=True, vmem_limit_bytes=VMEM_LIMIT
        ),
        name="k3_backward",
    )(*args)


def k4_kernel(g, out, slots, ss, sr):
    pc = Place()
    me = pc.w * 4 + pc.n
    bar = pltpu.get_barrier_semaphore()

    @pl.loop(1, 32)
    def _(j):
        t = (me + j) % 32
        pl.semaphore_signal(bar, inc=1, device_id=(t // 4, t % 4), device_id_type=MESH)

    pl.semaphore_wait(bar, 31)

    @pl.loop(1, 32)
    def _(j):
        t = (me + j) % 32
        remote(g.at[t], slots.at[me], ss.at[t], sr.at[me], (t // 4, t % 4)).start()

    slots[me] = g[me]

    @pl.loop(1, 32)
    def _(j):
        t = (me + j) % 32
        f = (me + 32 - j) % 32
        cp = remote(g.at[t], slots.at[f], ss.at[t], sr.at[f], (t // 4, t % 4))
        cp.wait_send()
        cp.wait_recv()

    out[...] = jnp.sum(slots[...], axis=0)


def k4_call(g):
    return pl.pallas_call(
        k4_kernel,
        out_shape=jax.ShapeDtypeStruct((8, 128), f32),
        in_specs=[VMEM],
        out_specs=VMEM,
        scratch_shapes=[
            pltpu.VMEM((32, 8, 128), f32),
            pltpu.SemaphoreType.DMA((32,)),
            pltpu.SemaphoreType.DMA((32,)),
        ],
        compiler_params=pltpu.CompilerParams(collective_id=3, has_side_effects=True),
        name="k4_vectors",
    )(g)


def chip_body(tokens, cotangent, bucket_counts, *params):
    core = lax.axis_index(AXES[0]) % 2
    tok2, vec, eb, lb, db, vb, md, ml, mvo, mf = prepare(tokens, *params)
    vec = jnp.pad(vec, ((0, 1), (0, 0)))
    ovo, _, _, ef, nrm, val, hid, slo, atl, atm, ats, wa, la, mix, vv = k1_call(
        tokens, tok2, vec, db, lb, vb, mvo, md, ml, mf
    )
    lay, gres, gmix, dff, dout, sums = k2_call(tokens, cotangent, bucket_counts, mix, ovo, ef, vec, eb)
    tg, od, ol, ofe, dvo, dbs, lbs, vbs, ags = k3_call(
        dff, dout, nrm, val, gmix, hid, slo, atl, atm, ats, wa, la, vv, tokens, gres, vec
    )
    vb_all = lax.dynamic_update_slice(jnp.zeros((1, D), f32), vbs[0:1], (0, HALF * core))
    lb_all = lax.dynamic_update_slice(jnp.zeros((HEADS, L3), f32), lbs[0:6], (6 * core, 0))
    db_all = lax.dynamic_update_slice(jnp.zeros((HEADS, HIDDEN_SIZE), f32), dbs[0:6], (6 * core, 0))
    v7 = jnp.concatenate([ags[0:2], vb_all, sums[3:4], sums[0:2], sums[2:3]])
    pack = jnp.concatenate(
        [
            v7.reshape(7, 32, 24).transpose(1, 0, 2).reshape(32, 168),
            sums[4:8].reshape(32, 96),
            lb_all.reshape(32, 192),
            db_all.reshape(32, 288),
            jnp.zeros((32, 1024 - 744), f32),
        ],
        axis=1,
    )
    red = k4_call(pack.reshape(32, 8, 128)).reshape(1024)
    small = lambda i: red[24 * i : 24 * i + 24]
    return (
        lay,
        tg,
        small(0),
        small(1),
        od.reshape(HEADS, 24, HIDDEN_SIZE),
        red[456:744],
        ol.reshape(HEADS, 24, L3),
        red[264:456],
        dvo[:, 0:24].transpose(1, 0, 2).reshape(24, D),
        small(2),
        dvo[:, 24:48].transpose(1, 0, 2).reshape(24, D),
        small(3),
        small(4),
        small(5),
        ofe[0].reshape(4, 24, D).transpose(1, 0, 2).reshape(24, 4 * D),
        red[168:264],
        ofe[1].reshape(96, D),
        small(6),
    )


def smooth_gate(values_in):
    return (
        0.5
        * values_in
        * (1.0 + jnp.tanh(gelu_root * (values_in + gelu_cube * values_in * values_in * values_in)))
    )


def gate_slope(values_in):
    squared = values_in * values_in
    tangent = jnp.tanh(gelu_root * (values_in + gelu_cube * squared * values_in))
    return 0.5 * (1.0 + tangent) + 0.5 * values_in * (1.0 - tangent * tangent) * gelu_root * (
        1.0 + 3.0 * gelu_cube * squared
    )


def bucket_layout():
    return ((S1, L1), (S2, L2), (S3, L3))


def live_rows(counts):
    pieces = []
    for bucket_index, (slot_count, seq_length) in enumerate(bucket_layout()):
        slot_of_row = jnp.arange(slot_count * seq_length, dtype=jnp.int32) // seq_length
        pieces.append(jnp.where(slot_of_row < counts[bucket_index], 1.0, 0.0).astype(jnp.float32))
    return jnp.concatenate(pieces)


def product(left_side, right_side):
    return jnp.dot(left_side, right_side, preferred_element_type=jnp.float32)


def column_sums(matrix_rows):
    return jnp.sum(matrix_rows.astype(jnp.float32), axis=0)


def norm_forward(inputs_float, norm_gain, norm_shift):
    row_mean = jnp.mean(inputs_float, axis=-1, keepdims=True)
    centred = inputs_float - row_mean
    inverse_scale = lax.rsqrt(jnp.mean(centred * centred, axis=-1, keepdims=True) + norm_eps)
    unit_rows = centred * inverse_scale
    return (unit_rows * norm_gain + norm_shift, unit_rows, inverse_scale)


def norm_backward(grad_normed, unit_rows, inverse_scale, norm_gain):
    grad_unit = grad_normed * norm_gain
    grad_inputs = inverse_scale * (
        grad_unit
        - jnp.mean(grad_unit, axis=-1, keepdims=True)
        - unit_rows * jnp.mean(grad_unit * unit_rows, axis=-1, keepdims=True)
    )
    return (grad_inputs, jnp.sum(grad_normed * unit_rows, axis=0), jnp.sum(grad_normed, axis=0))


def forward_pass(tokens, live_mask, gathered):
    (
        attn_gain,
        attn_shift,
        dense_weight,
        dense_bias,
        logit_weight,
        logit_bias,
        value_weight,
        value_bias,
        output_weight,
        output_bias,
        feed_gain,
        feed_shift,
        expand_weight,
        expand_bias,
        reduce_weight,
        reduce_bias,
    ) = gathered
    inputs_float = tokens.astype(jnp.float32)
    normed_float, unit_one, scale_one = norm_forward(
        inputs_float, attn_gain.astype(jnp.float32), attn_shift.astype(jnp.float32)
    )
    normed = normed_float.astype(jnp.bfloat16)
    values = (product(normed, value_weight) + value_bias.astype(jnp.float32)).astype(jnp.bfloat16)
    dense_heads = dense_bias.astype(jnp.float32).reshape(HEADS, 1, HIDDEN_SIZE)
    logit_heads = logit_bias.astype(jnp.float32).reshape(HEADS, 1, L3)
    pre_list, hidden_list, attention_list, mixed_list = ([], [], [], [])
    start_row = 0
    for slot_count, seq_length in bucket_layout():
        stop_row = start_row + slot_count * seq_length
        pre_act = (
            jnp.einsum(
                "rd,hde->hre",
                normed[start_row:stop_row],
                dense_weight,
                preferred_element_type=jnp.float32,
            )
            + dense_heads
        )
        hidden = smooth_gate(pre_act).astype(jnp.bfloat16)
        scores = (
            jnp.einsum(
                "hre,hel->hrl",
                hidden,
                logit_weight[:, :, :seq_length],
                preferred_element_type=jnp.float32,
            )
            + logit_heads[:, :, :seq_length]
        )
        attention = jax.nn.softmax(scores, axis=-1)
        attention_low = attention.astype(jnp.bfloat16).reshape(
            HEADS, slot_count, seq_length, seq_length
        )
        block_values = values[start_row:stop_row].reshape(slot_count, seq_length, HEADS, HEAD_DIM)
        mixed_heads = jnp.einsum(
            "hsql,slhc->sqhc", attention_low, block_values, preferred_element_type=jnp.float32
        )
        mixed_list.append(mixed_heads.reshape(slot_count * seq_length, D))
        pre_list.append(pre_act)
        hidden_list.append(hidden)
        attention_list.append(attention)
        start_row = stop_row
    mixed_all = jnp.concatenate(mixed_list, axis=0).astype(jnp.bfloat16)
    attended = product(mixed_all, output_weight) + output_bias.astype(jnp.float32)
    residual = inputs_float + attended
    normed_two_float, unit_two, scale_two = norm_forward(
        residual, feed_gain.astype(jnp.float32), feed_shift.astype(jnp.float32)
    )
    normed_two = normed_two_float.astype(jnp.bfloat16)
    expand_pre = product(normed_two, expand_weight) + expand_bias.astype(jnp.float32)
    inner_act = smooth_gate(expand_pre).astype(jnp.bfloat16)
    feed_out = product(inner_act, reduce_weight) + reduce_bias.astype(jnp.float32)
    layer_out = live_mask[:, None] * (residual + feed_out)
    stored = (
        normed,
        unit_one,
        scale_one,
        values,
        pre_list,
        hidden_list,
        attention_list,
        mixed_all,
        unit_two,
        scale_two,
        normed_two,
        expand_pre,
        inner_act,
    )
    return (layer_out, stored)


def backward_pass(cotangent, live_mask, gathered, stored):
    (
        attn_gain,
        attn_shift,
        dense_weight,
        dense_bias,
        logit_weight,
        logit_bias,
        value_weight,
        value_bias,
        output_weight,
        output_bias,
        feed_gain,
        feed_shift,
        expand_weight,
        expand_bias,
        reduce_weight,
        reduce_bias,
    ) = gathered
    (
        normed,
        unit_one,
        scale_one,
        values,
        pre_list,
        hidden_list,
        attention_list,
        mixed_all,
        unit_two,
        scale_two,
        normed_two,
        expand_pre,
        inner_act,
    ) = stored
    grad_out = cotangent.astype(jnp.float32) * live_mask[:, None]
    grad_feed = grad_out.astype(jnp.bfloat16)
    reduce_weight_grad = jnp.einsum(
        "rf,rd->fd", inner_act, grad_feed, preferred_element_type=jnp.float32
    )
    reduce_bias_grad = column_sums(grad_feed)
    grad_inner = jnp.einsum(
        "rd,fd->rf", grad_feed, reduce_weight, preferred_element_type=jnp.float32
    )
    grad_expand = (grad_inner * gate_slope(expand_pre)).astype(jnp.bfloat16)
    expand_weight_grad = jnp.einsum(
        "rd,rf->df", normed_two, grad_expand, preferred_element_type=jnp.float32
    )
    expand_bias_grad = column_sums(grad_expand)
    grad_normed_two = jnp.einsum(
        "rf,df->rd", grad_expand, expand_weight, preferred_element_type=jnp.float32
    )
    grad_residual_norm, feed_gain_grad, feed_shift_grad = norm_backward(
        grad_normed_two, unit_two, scale_two, feed_gain.astype(jnp.float32)
    )
    grad_residual = grad_out + grad_residual_norm
    grad_attended = grad_residual.astype(jnp.bfloat16)
    output_weight_grad = jnp.einsum(
        "rd,re->de", mixed_all, grad_attended, preferred_element_type=jnp.float32
    )
    output_bias_grad = column_sums(grad_attended)
    grad_mixed = jnp.einsum(
        "re,de->rd", grad_attended, output_weight, preferred_element_type=jnp.float32
    ).astype(jnp.bfloat16)
    dense_weight_grad = jnp.zeros((HEADS, D, HIDDEN_SIZE), jnp.float32)
    dense_bias_grad = jnp.zeros((HEADS, HIDDEN_SIZE), jnp.float32)
    logit_weight_grad = jnp.zeros((HEADS, HIDDEN_SIZE, L3), jnp.float32)
    logit_bias_grad = jnp.zeros((HEADS, L3), jnp.float32)
    grad_normed_list, value_sum_list = ([], [])
    start_row = 0
    for bucket_index, (slot_count, seq_length) in enumerate(bucket_layout()):
        row_count = slot_count * seq_length
        stop_row = start_row + row_count
        attention = attention_list[bucket_index]
        hidden = hidden_list[bucket_index]
        pre_act = pre_list[bucket_index]
        attention_low = attention.astype(jnp.bfloat16).reshape(
            HEADS, slot_count, seq_length, seq_length
        )
        block_values = values[start_row:stop_row].reshape(slot_count, seq_length, HEADS, HEAD_DIM)
        block_grad = grad_mixed[start_row:stop_row].reshape(slot_count, seq_length, HEADS, HEAD_DIM)
        grad_attention = jnp.einsum(
            "sqhc,slhc->hsql", block_grad, block_values, preferred_element_type=jnp.float32
        ).reshape(HEADS, row_count, seq_length)
        value_sum_list.append(
            jnp.einsum(
                "hsql,sqhc->slhc", attention_low, block_grad, preferred_element_type=jnp.float32
            ).reshape(row_count, D)
        )
        grad_scores = (
            attention
            * (grad_attention - jnp.sum(attention * grad_attention, axis=-1, keepdims=True))
        ).astype(jnp.bfloat16)
        logit_weight_grad = logit_weight_grad.at[:, :, :seq_length].add(
            jnp.einsum("hre,hrl->hel", hidden, grad_scores, preferred_element_type=jnp.float32)
        )
        logit_bias_grad = logit_bias_grad.at[:, :seq_length].add(
            jnp.sum(grad_scores.astype(jnp.float32), axis=1)
        )
        grad_hidden = jnp.einsum(
            "hrl,hel->hre",
            grad_scores,
            logit_weight[:, :, :seq_length],
            preferred_element_type=jnp.float32,
        )
        grad_dense = (grad_hidden * gate_slope(pre_act)).astype(jnp.bfloat16)
        dense_weight_grad = dense_weight_grad + jnp.einsum(
            "rd,hre->hde",
            normed[start_row:stop_row],
            grad_dense,
            preferred_element_type=jnp.float32,
        )
        dense_bias_grad = dense_bias_grad + jnp.sum(grad_dense.astype(jnp.float32), axis=1)
        grad_normed_list.append(
            jnp.einsum("hre,hde->rd", grad_dense, dense_weight, preferred_element_type=jnp.float32)
        )
        start_row = stop_row
    grad_values = jnp.concatenate(value_sum_list, axis=0).astype(jnp.bfloat16)
    value_weight_grad = jnp.einsum(
        "rd,re->de", normed, grad_values, preferred_element_type=jnp.float32
    )
    value_bias_grad = column_sums(grad_values)
    grad_normed = jnp.concatenate(grad_normed_list, axis=0) + jnp.einsum(
        "re,de->rd", grad_values, value_weight, preferred_element_type=jnp.float32
    )
    grad_inputs_norm, attn_gain_grad, attn_shift_grad = norm_backward(
        grad_normed, unit_one, scale_one, attn_gain.astype(jnp.float32)
    )
    tokens_grad = grad_residual + grad_inputs_norm
    return (
        tokens_grad,
        (
            attn_gain_grad,
            attn_shift_grad,
            dense_weight_grad,
            dense_bias_grad.reshape(-1),
            logit_weight_grad,
            logit_bias_grad.reshape(-1),
            value_weight_grad,
            value_bias_grad,
            output_weight_grad,
            output_bias_grad,
            feed_gain_grad,
            feed_shift_grad,
            expand_weight_grad,
            expand_bias_grad,
            reduce_weight_grad,
            reduce_bias_grad,
        ),
    )


def body(
    tokens,
    cotangent,
    bucket_counts,
    attn_gain,
    attn_shift,
    dense_weight,
    dense_bias,
    logit_weight,
    logit_bias,
    value_weight,
    value_bias,
    output_weight,
    output_bias,
    feed_gain,
    feed_shift,
    expand_weight,
    expand_bias,
    reduce_weight,
    reduce_bias,
):
    gathered = (
        lax.all_gather(attn_gain, AXES, axis=0, tiled=True),
        lax.all_gather(attn_shift, AXES, axis=0, tiled=True),
        lax.all_gather(dense_weight, AXES, axis=1, tiled=True),
        lax.all_gather(dense_bias, AXES, axis=0, tiled=True),
        lax.all_gather(logit_weight, AXES, axis=1, tiled=True),
        lax.all_gather(logit_bias, AXES, axis=0, tiled=True),
        lax.all_gather(value_weight, AXES, axis=0, tiled=True),
        lax.all_gather(value_bias, AXES, axis=0, tiled=True),
        lax.all_gather(output_weight, AXES, axis=0, tiled=True),
        lax.all_gather(output_bias, AXES, axis=0, tiled=True),
        lax.all_gather(feed_gain, AXES, axis=0, tiled=True),
        lax.all_gather(feed_shift, AXES, axis=0, tiled=True),
        lax.all_gather(expand_weight, AXES, axis=0, tiled=True),
        lax.all_gather(expand_bias, AXES, axis=0, tiled=True),
        lax.all_gather(reduce_weight, AXES, axis=0, tiled=True),
        lax.all_gather(reduce_bias, AXES, axis=0, tiled=True),
    )
    live_mask = live_rows(bucket_counts[0])
    layer_out, stored = forward_pass(tokens, live_mask, gathered)
    gathered = (
        lax.all_gather(attn_gain, AXES, axis=0, tiled=True),
        lax.all_gather(attn_shift, AXES, axis=0, tiled=True),
        lax.all_gather(dense_weight, AXES, axis=1, tiled=True),
        lax.all_gather(dense_bias, AXES, axis=0, tiled=True),
        lax.all_gather(logit_weight, AXES, axis=1, tiled=True),
        lax.all_gather(logit_bias, AXES, axis=0, tiled=True),
        lax.all_gather(value_weight, AXES, axis=0, tiled=True),
        lax.all_gather(value_bias, AXES, axis=0, tiled=True),
        lax.all_gather(output_weight, AXES, axis=0, tiled=True),
        lax.all_gather(output_bias, AXES, axis=0, tiled=True),
        lax.all_gather(feed_gain, AXES, axis=0, tiled=True),
        lax.all_gather(feed_shift, AXES, axis=0, tiled=True),
        lax.all_gather(expand_weight, AXES, axis=0, tiled=True),
        lax.all_gather(expand_bias, AXES, axis=0, tiled=True),
        lax.all_gather(reduce_weight, AXES, axis=0, tiled=True),
        lax.all_gather(reduce_bias, AXES, axis=0, tiled=True),
    )
    tokens_grad, grads = backward_pass(cotangent, live_mask, gathered, stored)
    shards = (
        lax.psum_scatter(grads[0], AXES, scatter_dimension=0, tiled=True),
        lax.psum_scatter(grads[1], AXES, scatter_dimension=0, tiled=True),
        lax.psum_scatter(grads[2], AXES, scatter_dimension=1, tiled=True),
        lax.psum_scatter(grads[3], AXES, scatter_dimension=0, tiled=True),
        lax.psum_scatter(grads[4], AXES, scatter_dimension=1, tiled=True),
        lax.psum_scatter(grads[5], AXES, scatter_dimension=0, tiled=True),
        lax.psum_scatter(grads[6], AXES, scatter_dimension=0, tiled=True),
        lax.psum_scatter(grads[7], AXES, scatter_dimension=0, tiled=True),
        lax.psum_scatter(grads[8], AXES, scatter_dimension=0, tiled=True),
        lax.psum_scatter(grads[9], AXES, scatter_dimension=0, tiled=True),
        lax.psum_scatter(grads[10], AXES, scatter_dimension=0, tiled=True),
        lax.psum_scatter(grads[11], AXES, scatter_dimension=0, tiled=True),
        lax.psum_scatter(grads[12], AXES, scatter_dimension=0, tiled=True),
        lax.psum_scatter(grads[13], AXES, scatter_dimension=0, tiled=True),
        lax.psum_scatter(grads[14], AXES, scatter_dimension=0, tiled=True),
        lax.psum_scatter(grads[15], AXES, scatter_dimension=0, tiled=True),
    )
    return (layer_out, tokens_grad) + tuple(shards)


def solution(mesh):
    in_specs = (
        P(AXES, None),
        P(AXES, None),
        P(AXES, None),
        P(AXES),
        P(AXES),
        P(None, AXES, None),
        P(AXES),
        P(None, AXES, None),
        P(AXES),
        P(AXES, None),
        P(AXES),
        P(AXES, None),
        P(AXES),
        P(AXES),
        P(AXES),
        P(AXES, None),
        P(AXES),
        P(AXES, None),
        P(AXES),
    )
    out_specs = (
        P(AXES, None),
        P(AXES, None),
        P(AXES),
        P(AXES),
        P(None, AXES, None),
        P(AXES),
        P(None, AXES, None),
        P(AXES),
        P(AXES, None),
        P(AXES),
        P(AXES, None),
        P(AXES),
        P(AXES),
        P(AXES),
        P(AXES, None),
        P(AXES),
        P(AXES, None),
        P(AXES),
    )
    shape = tuple(mesh.shape[a] for a in AXES)
    chosen = chip_body if shape == (8, 4) else body
    return jax.shard_map(chosen, mesh=mesh, in_specs=in_specs, out_specs=out_specs, check_vma=False)
```

profile of v0, /device:TPU:0, one launch (start us, length us, event | category | flops | bytes accessed | tf_op | source)
XLA Modules:
  0.0 505.1 jit_solution(6596027403400740037)
XLA Ops:
  0.7 0.9 copy.58
  1.6 1.7 pad_maximum_fusion.ff
  3.3 0.8 stack_reshape.12
  4.0 0.8 stack_reshape.13
  5.5 7.4 %concatenate.10 = bf16[2048]{0:T(1024)(128)(2,1)} concatenate(bf16[24]{0:T(256)(128)(2,1)} %param.22, bf16[24]{0:T(256)(128)(2,1)} %param.23, bf16[24]{0:T(256)(128)(2,1)} %param.29, bf16[24]{0:T(256)(128)(2,1)} %param.31, bf16[24]{0:T(256)(128)(2,1)} %param.32, bf16[24]{0:T(256)(128)(2,1)} %param.33, bf16[24]{0:T(256)(128)(2,1)} %param.37, bf16[96]{0:T(256)(128)(2,1)} %param.35, ...), dimensions={0} | concatenate | bytes 8192 | tf_op jit(solution)/shard_map/concatenate | solution.py:594
  12.9 14.7 %k0_exchange.1 = (bf16[32,16,128]{2,1,0:T(8,128)(2,1)}, bf16[1024,768]{1,0:T(8,128)(2,1)}, bf16[3,2,48,768]{3,2,1,0:T(8,128)(2,1)}, bf16[3,2,48,512]{3,2,1,0:T(8...) custom-call(bf16[16,128]{1,0:T(8,128)(2,1)} %bitcast.66, bf16[1024,768]{1,0:T(8,128)(2,1)} %tok.3, ...), custom_call_target="tpu_custom_call" | custom-call | tf_op jit(solution)/shard_map/k0_exchange/pallas_call | solution.py:145
  27.6 0.9 copy.59
  31.7 184.9 %k1_attention.1 = (bf16[2,4,2,4,48,384]{5,4,3,2,1,0:T(8,128)(2,1)}, bf16[3,4,2,4,48,768]{5,4,3,2,1,0:T(8,128)(2,1)}, bf16[3,4,2,4,48,512]{5,4,3,2,1,0:T(8,128)(2...) custom-call(bf16[1024,768]{1,0:T(8,128)(2,1)} %tok.3, ...), custom_call_target="tpu_custom_call" | custom-call | tf_op jit(solution)/shard_map/k1_attention/pallas_call | solution.py:543
  217.4 55.9 %k2_feed.1 = (f32[1024,768]{1,0:T(8,128)}, f32[1024,768]{1,0:T(8,128)}, bf16[2,1024,384]{2,1,0:T(8,128)(2,1)}, bf16[2,2,4,2,4,48,768]{6,5,4,3,2,1,0:T(8,128)(2,1...) custom-call(bf16[1024,768]{1,0:T(8,128)(2,1)} %tok.3, bf16[1024,768]{1,0:T(8,128)(2,1)} %cot.1, ...), custom_call_target="tpu_custom_call" | custom-call | tf_op jit(solution)/shard_map/k2_feed/pallas_call | solution.py:746
  273.3 198.8 %k3_backward.1 = (f32[1024,768]{1,0:T(8,128)}, f32[6,48,768]{2,1,0:T(8,128)}, f32[6,48,512]{2,1,0:T(8,128)}, f32[2,2,48,768]{3,2,1,0:T(8,128)}, f32[2,48,384]{2,...) custom-call(bf16[2,2,4,2,4,48,768]{6,5,4,3,2,1,0:T(8,128)(2,1)} %get-tuple-element.62.d, ...), custom_call_target="tpu_custom_call" | custom-call | tf_op jit(solution)/shard_map/k3_backward/pallas_call | solution.py:1222
  472.2 0.9 slice_dynamic-update-slice_fusion
  473.0 0.9 slice.93
  474.9 0.9 dynamic_update_slice.11
  475.9 0.9 dynamic_update_slice.10
  478.3 0.9 concatenate.12
  479.8 12.0 %k4_vectors.1 = f32[8,128]{1,0:T(8,128)} custom-call(f32[32,8,128]{2,1,0:T(8,128)} %bitcast.48), custom_call_target="tpu_custom_call" | custom-call | tf_op jit(solution)/shard_map/k4_vectors/pallas_call | solution.py:1305
  491.9 1.5 fusion.1
  493.4 1.3 slice.102
  494.7 1.3 slice.103
  496.0 1.3 slice.111
  497.3 1.8 fusion
  501.1 1.7 copy.66
  502.9 0.9 copy.67
  503.8 0.8 copy.68
  (50 shorter events, 9.9 us)
Async XLA Ops:
  273.3 200.6 %copy-start.4 = (f32[8,768]{1,0:T(8,128)S(1)}, f32[8,768]{1,0:T(8,128)}, u32[]{:S(2)}) copy-start(f32[8,768]{1,0:T(8,128)} %get-tuple-element.79) | copy-start | bytes 73732
  472.1 27.7 %copy-start.3 = (f32[2,48,384]{2,1,0:T(8,128)S(1)}, f32[2,48,384]{2,1,0:T(8,128)}, u32[]{:S(2)}) copy-start(f32[2,48,384]{2,1,0:T(8,128)} %get-tuple-element.84) | copy-start | bytes 442372
  472.2 29.0 %copy-start = (f32[1024,768]{1,0:T(8,128)S(1)}, f32[1024,768]{1,0:T(8,128)}, u32[]{:S(2)}) copy-start(f32[1024,768]{1,0:T(8,128)} %get-tuple-element.116) | copy-start | bytes 9437188
  501.1 1.8 copy-start.1
  501.1 2.7 copy-start.2
where the time goes:
time: 509 us; the launch traced here: 505 us
  Pallas kernels  466 us (92%)
  local copies, waits for them, and re-layouts  35 us (7%)
    pallas_call x1, Pallas kernels, k3_call(): pl.pallas_call(k3_kernel, out_shape=(sds((ROWS_DEV, D), f32), sds((6, 48,...  199 us
    pallas_call x1, Pallas kernels, k1_call(): pl.pallas_call(k1_kernel, out_shape=(sds((2, 4, 2, 4, 48, HALF), bf16), s...  185 us
    pallas_call x1, Pallas kernels, k2_call(): pl.pallas_call(k2_kernel, out_shape=(sds((ROWS_DEV, D), f32), sds((ROWS_D...  55.9 us
    pallas_call x1, Pallas kernels, k0_call(): pl.pallas_call(k0_kernel, out_shape=(sds((32, 16, 128), bf16), sds((ROWS_...  14.7 us
    pallas_call x1, Pallas kernels, k4_call(): pl.pallas_call(k4_kernel, out_shape=jax.ShapeDtypeStruct((8, 128), f32),...  12 us

commit v1 on v0

--- a/solution.py
+++ b/solution.py
@@ -218,7 +218,8 @@
         self.ycopy(k, buf, zz, col=pc.ny).wait_recv()
         self.dcopy(k, buf, zz).start()
 
-    def fin(self, k, src, buf):
+    def fin(self, k, src, buf, each=None):
+        self.own(k, src, buf).wait()
         for zz in range(4):
             remote(
                 buf.at[zz, :, self.pc.nd],
@@ -227,7 +228,8 @@
                 self.dr.at[k, zz],
                 self.pc.xdev,
             ).wait_recv()
-        self.own(k, src, buf).wait()
+            if each is not None:
+                each(zz)
 
     def sent(self, k, src, buf):
         for i in (1, 2, 3):
@@ -236,6 +238,103 @@
             self.xcopy(k, buf, zz).wait_send()
             self.ycopy(k, buf, zz).wait_send()
             self.dcopy(k, buf, zz).wait_send()
+
+
+class LayerFirst:
+    def __init__(self, pc, src, buf, cs, cr, us, ur, vs, vr, ls, ps, pr):
+        self.pc, self.src, self.buf = pc, src, buf
+        self.cs, self.cr, self.us, self.ur, self.vs, self.vr, self.ls = cs, cr, us, ur, vs, vr, ls
+        self.ps, self.pr = ps, pr
+
+    def side(self, i, src, slot):
+        dev = self.pc.xdev if i in (0, 3) else self.pc.ydev
+        return remote(src, slot, self.cs.at[i], self.cr.at[i], dev)
+
+    def local(self):
+        return pltpu.make_async_copy(self.src, self.buf.at[self.pc.z, :, self.pc.n], self.ls)
+
+    def first(self):
+        pc = self.pc
+        self.local().start()
+        for i in (0, 1):
+            self.side(i, self.src, self.buf.at[pc.z, :, pc.n]).start()
+
+    def halves(self):
+        pc = self.pc
+        a, b = self.buf.at[pc.z, 0, pc.nx], self.buf.at[pc.z, 1, pc.ny]
+        return self.side(2, a, a), self.side(3, b, b)
+
+    def second(self):
+        for i in (0, 1):
+            self.side(i, self.src, self.buf.at[self.pc.z, :, self.pc.n]).wait_recv()
+        for cp in self.halves():
+            cp.start()
+
+    def up(self, r):
+        return remote(self.buf.at[r], self.buf.at[r], self.us.at[r], self.ur.at[r], self.pc.zdev((self.pc.z + 1) % 4))
+
+    def down(self, r):
+        return remote(self.buf.at[r], self.buf.at[r], self.vs.at[r], self.vr.at[r], self.pc.zdev((self.pc.z + 3) % 4))
+
+    def swap(self, r):
+        return remote(self.buf.at[r], self.buf.at[r], self.ps.at[r], self.pr.at[r], self.pc.sib)
+
+    def third(self):
+        z = self.pc.z
+        for cp in self.halves():
+            cp.wait_recv()
+        self.local().wait()
+
+        @pl.when(z < 3)
+        def _():
+            self.up(z).start()
+
+        @pl.when(z > 0)
+        def _():
+            self.down(z).start()
+
+        self.swap(z).start()
+
+    def level(self, k):
+        z = self.pc.z
+
+        @pl.when(z >= k)
+        def _():
+            self.up(z - k).wait_recv()
+
+            @pl.when(z < 3)
+            def _():
+                self.up(z - k).start()
+
+            self.swap(z - k).start()
+
+        @pl.when(z + k <= 3)
+        def _():
+            self.down(z + k).wait_recv()
+
+            @pl.when(z > 0)
+            def _():
+                self.down(z + k).start()
+
+            self.swap(z + k).start()
+
+    def finish(self):
+        z = self.pc.z
+        for i in (0, 1):
+            self.side(i, self.src, self.buf.at[self.pc.z, :, self.pc.n]).wait_send()
+        for cp in self.halves():
+            cp.wait_send()
+        for r in range(4):
+
+            @pl.when((z < 3) & (z >= r))
+            def _():
+                self.up(r).wait_send()
+
+            @pl.when((z > 0) & (z <= r))
+            def _():
+                self.down(r).wait_send()
+
+            self.swap(r).wait()
 
 
 def gather_sems(k):
@@ -263,6 +362,7 @@
     ovo, gd, gl, ef, nrm_o, val_o, hid_o, slo_o, atl_o, atm_o, ats_o, wa_o, la_o, mix_o, vv_o,
     tokv, nrm, val, vst, vv, wst, lst, wv, lv, hidv, slov, atlv, atmv, atsv, mixv,
     zs, zr, xs, xr, ys, yr, ds, dr, ls, tsem, osem, wsem, lsem, ssem, rsem, msem,
+    cs, cr, us, ur, vs, vr, cls, ps, pr,
 ):
     pc = Place()
     c = pc.c
@@ -279,18 +379,15 @@
     vo_args = (0, mvo, ovo.at[c])
     dd = lambda p: (1 + 2 * p, md.at[p], gd.at[p])
     ll = lambda p: (2 + 2 * p, ml.at[p], gl.at[p])
-    fa = (7, mf.at[0], ef.at[c, 0])
-    fb = (8, mf.at[1], ef.at[c, 1])
+    fb = (7, mf.at[1], ef.at[c, 1])
+    fa = LayerFirst(pc, mf.at[0], ef.at[c, 0], cs, cr, us, ur, vs, vr, cls, ps, pr)
 
     g.zsend(*vo_args)
     g.zsend(*dd(0))
-    for i in range(4):
-        g.col(*vo_args, i)
-    g.zsend(*ll(0))
-    for i in range(4):
-        g.col(*dd(0), i)
-    for zz in range(4):
-        g.diag(vo_args[0], vo_args[2], zz)
+    g.col(*vo_args, 0)
+    g.col(*dd(0), 0)
+    fa.first()
+    g.col(*ll(0), 0)
 
     for cp in tcopies:
         cp.wait()
@@ -303,9 +400,23 @@
 
     nrm_copy = pltpu.make_async_copy(nrm, nrm_o, tsem.at[4])
     nrm_copy.start()
+    for i in (1, 2, 3):
+        g.col(*vo_args, i)
+    g.zsend(*ll(0))
+    fa.second()
+    g.col(*dd(1), 0)
+    for i in (1, 2, 3):
+        g.col(*dd(0), i)
     g.zsend(*dd(1))
-    for i in range(4):
+    fa.third()
+    for zz in range(4):
+        g.diag(vo_args[0], vo_args[2], zz)
+    g.col(*ll(1), 0)
+    for i in (1, 2, 3):
         g.col(*ll(0), i)
+    g.zsend(*ll(1))
+    for zz in (0, 2, 1, 3):
+        g.diag(dd(0)[0], dd(0)[2], zz)
     g.fin(*vo_args)
     vo_load = pltpu.make_async_copy(ovo.at[c], vst, tsem.at[5])
     vo_load.start()
@@ -327,12 +438,8 @@
     val_copy.start()
     vv_copy = pltpu.make_async_copy(vv, vv_o, tsem.at[5])
     vv_copy.start()
-    for zz in range(4):
-        g.diag(dd(0)[0], dd(0)[2], zz)
-    g.zsend(*ll(1))
-    for i in range(2):
-        g.col(*dd(1), i)
-    for zz in range(4):
+    g.col(*dd(1), 1)
+    for zz in (0, 2, 1, 3):
         g.diag(ll(0)[0], ll(0)[2], zz)
     g.fin(*dd(0))
     g.fin(*ll(0))
@@ -358,17 +465,13 @@
 
             @pl.when(jnp.logical_not(more))
             def _():
-                fn(*fa)
+                fn(*fb)
 
         def on_b(fn):
             @pl.when(more)
             def _():
                 fn(kb, ml.at[q % 3], gl.at[q % 3])
 
-            @pl.when(jnp.logical_not(more))
-            def _():
-                fn(*fb)
-
         def on_next(fn):
             @pl.when(p == 0)
             def _():
@@ -376,41 +479,42 @@
 
             @pl.when(p == 1)
             def _():
-                fn(*fa)
+                fn(*fb)
 
         def on_next_b(fn):
             @pl.when(p == 0)
             def _():
                 fn(6, ml.at[2], gl.at[2])
 
-            @pl.when(p == 1)
-            def _():
-                fn(*fb)
-
         def tick(pos):
             if pos == 0:
+                on_next(lambda k, s, b: g.col(k, s, b, 0))
                 on_a(lambda k, s, b: g.col(k, s, b, 2))
                 on_a(lambda k, s, b: g.col(k, s, b, 3))
                 on_next(g.zsend)
             elif pos == 1:
-                on_b(lambda k, s, b: g.col(k, s, b, 0))
                 on_b(lambda k, s, b: g.col(k, s, b, 1))
+                on_b(lambda k, s, b: g.col(k, s, b, 2))
             elif pos == 2:
+                on_b(lambda k, s, b: g.col(k, s, b, 3))
+                on_next_b(lambda k, s, b: g.col(k, s, b, 0))
+            elif pos == 3:
                 on_a(lambda k, s, b: g.diag(k, b, 0))
                 on_a(lambda k, s, b: g.diag(k, b, 2))
-            elif pos == 3:
-                on_b(lambda k, s, b: g.col(k, s, b, 2))
-                on_b(lambda k, s, b: g.col(k, s, b, 3))
+                for r in range(3):
+
+                    @pl.when(p == r)
+                    def _():
+                        fa.level(r + 1)
             elif pos == 4:
                 on_a(lambda k, s, b: g.diag(k, b, 1))
                 on_a(lambda k, s, b: g.diag(k, b, 3))
                 on_next_b(g.zsend)
             elif pos == 5:
-                on_next(lambda k, s, b: g.col(k, s, b, 0))
+                on_next(lambda k, s, b: g.col(k, s, b, 1))
                 on_b(lambda k, s, b: g.diag(k, b, 0))
             elif pos == 6:
                 on_b(lambda k, s, b: g.diag(k, b, 2))
-                on_next(lambda k, s, b: g.col(k, s, b, 1))
             elif pos == 7:
                 on_b(lambda k, s, b: g.diag(k, b, 1))
                 on_b(lambda k, s, b: g.diag(k, b, 3))
@@ -503,7 +607,11 @@
                     tick(pos)
                     pos += 1
                 mixv[rows, lanes] = mixed.astype(bf16)
-        on_a(g.fin)
+
+        @pl.when(more)
+        def _():
+            g.fin(ka, md.at[q % 3], gd.at[q % 3])
+
         on_b(g.fin)
 
         @pl.when(p == 2)
@@ -514,8 +622,8 @@
             wcopy(p).wait()
             lcopy(p).wait()
 
-    swaps = [remote(ef.at[c], ef.at[c], ssem.at[1], rsem.at[1], pc.sib), vo_swap]
-    swaps[0].start()
+    fb_swap = lambda r: remote(ef.at[c, 1, r], ef.at[c, 1, r], ssem.at[4 + r], rsem.at[4 + r], pc.sib)
+    swaps = [vo_swap]
     o = 1 - c
     for i, (start, to) in enumerate(((0, 512), (1024, 0))):
         mine = pltpu.make_async_copy(
@@ -527,13 +635,14 @@
         )
         other.start()
         swaps += [mine, other]
-    for cp in swaps + [nrm_copy, val_copy, vv_copy]:
+    g.fin(*fb, each=lambda r: fb_swap(r).start())
+    for cp in swaps + [nrm_copy, val_copy, vv_copy] + [fb_swap(r) for r in range(4)]:
         cp.wait()
+    fa.finish()
     g.sent(*vo_args)
     for p in range(3):
         g.sent(*dd(p))
         g.sent(*ll(p))
-    g.sent(*fa)
     g.sent(*fb)
 
 
@@ -578,8 +687,10 @@
             pltpu.VMEM((2, 256, L1), bf16),
             pltpu.VMEM((CHIP_ROWS, HALF), bf16),
         ]
-        + gather_sems(9)
-        + [dma((9,)), dma((2, 5)), dma, dma, dma((4,)), dma((4,)), dma((2,))],
+        + gather_sems(8)
+        + [dma((9,)), dma((2, 5)), dma, dma, dma((8,)), dma((8,)), dma((2,))]
+        + [dma((4,))] * 6
+        + [dma, dma((4,)), dma((4,))],
         compiler_params=pltpu.CompilerParams(
             collective_id=1, has_side_effects=True, vmem_limit_bytes=VMEM_LIMIT
         ),
@@ -591,10 +702,12 @@
             value_bias, output_weight, output_bias, feed_gain, feed_shift, expand_weight, expand_bias,
             reduce_weight, reduce_bias):
     core = lax.axis_index(AXES[0]) % 2
+    narrow_rows = jnp.stack([attn_gain, attn_shift, value_bias, output_bias, feed_gain, feed_shift, reduce_bias])
+    wide_rows = [expand_bias.reshape(1, 96), logit_bias.reshape(2, 96), dense_bias.reshape(3, 96)]
     small = jnp.concatenate(
-        [attn_gain, attn_shift, value_bias, output_bias, feed_gain, feed_shift, reduce_bias,
-         expand_bias, logit_bias, dense_bias, jnp.zeros((2048 - 744,), bf16)]
-    ).reshape(16, 128)
+        [jnp.pad(narrow_rows, ((0, 0), (0, 104)))] + [jnp.pad(v, ((0, 0), (0, 32))) for v in wide_rows]
+    )
+    small = jnp.pad(small, ((0, 3), (0, 0)))
     dense = dense_weight.reshape(6, 48, D)
     logit = logit_weight.reshape(6, 48, L3)
     vo = jnp.stack([value_weight.reshape(24, 2, HALF), output_weight.reshape(24, 2, HALF)]).transpose(2, 0, 1, 3)
@@ -603,11 +716,11 @@
         [expand_weight.reshape(24, 4, D).transpose(1, 0, 2).reshape(2, 48, D), reduce_weight.reshape(2, 48, D)]
     )
     s_all, tok2, md, ml, mvo, mf = k0_call(small, tokens, dense, logit, vo, ff)
-    flat = s_all.reshape(32, 2048)[:, :744].astype(f32)
-    vec = flat[:, :168].reshape(32, 7, 24).transpose(1, 0, 2).reshape(7, D)
-    eb = flat[:, 168:264].reshape(4, D)
-    lb = lax.dynamic_slice(flat[:, 264:456].reshape(HEADS, L3), (6 * core, 0), (6, L3))
-    db = lax.dynamic_slice(flat[:, 456:744].reshape(HEADS, HIDDEN_SIZE), (6 * core, 0), (6, HIDDEN_SIZE))
+    every = s_all.astype(f32)
+    vec = every[:, 0:7, :24].transpose(1, 0, 2).reshape(7, D)
+    eb = every[:, 7, :96].reshape(4, D)
+    lb = lax.dynamic_slice(every[:, 8:10, :96].reshape(HEADS, L3), (6 * core, 0), (6, L3))
+    db = lax.dynamic_slice(every[:, 10:13, :96].reshape(HEADS, HIDDEN_SIZE), (6 * core, 0), (6, HIDDEN_SIZE))
     vb = lax.dynamic_slice(vec[2:3], (0, HALF * core), (1, HALF))
     return tok2, vec, eb, lb, db, vb, md, ml, mvo, mf
 
@@ -729,13 +842,16 @@
                 dst[f, j, i // 4, i % 4] = acc[j % 2, at : at + 48].astype(bf16)
     for f in range(2):
         out_copy(1, f).start()
-    zero = jnp.zeros((24, HALF), f32)
+    zero = jnp.zeros((24, 128), f32)
     for hh in range(2):
         acc[0, 0:HALF] = dot(mix[hh], ga[...], TN)
         for i in range(16):
             for half in range(2):
-                part = acc[0, i * 24 : i * 24 + 24, half * HALF : half * HALF + HALF]
-                do_o[half, 2 * hh + i // 8, (i // 4) % 2, i % 4] = jnp.concatenate([zero, part], axis=0).astype(bf16)
+                for r in range(3):
+                    at = half * HALF + r * 128
+                    part = acc[0, i * 24 : i * 24 + 24, at : at + 128]
+                    both = jnp.concatenate([zero, part], axis=0).astype(bf16)
+                    do_o[half, r, 2 * hh + i // 8, (i // 4) % 2, i % 4] = both
     for f in range(2):
         out_copy(1, f).wait()
 
@@ -750,7 +866,7 @@
             sds((ROWS_DEV, D), f32),
             sds((2, ROWS_DEV, HALF), bf16),
             sds((2, 2, 4, 2, 4, 48, D), bf16),
-            sds((2, 4, 2, 4, 48, HALF), bf16),
+            sds((2, 3, 4, 2, 4, 48, 128), bf16),
             sds((8, D), f32),
         ),
         in_specs=[VMEM, VMEM, pl.BlockSpec(memory_space=pltpu.SMEM), VMEM] + [HBM] * 2 + [VMEM] * 2,
@@ -796,11 +912,23 @@
             p5.at[zz, :, self.pc.n], bufs[3].at[i - 1], self.zs.at[k, i], self.zr.at[k, i], self.pc.zdev(zz)
         )
 
+    def row(self, k, p5, bufs, zz):
+        self.acopy(k, p5, bufs, zz).start()
+        (self.xcopy if zz < 2 else self.ycopy)(k, p5, bufs, zz).start()
+
     def one(self, k, p5, bufs):
-        for zz in range(4):
+        for zz in (0, 2, 1, 3):
             self.acopy(k, p5, bufs, zz).start()
-        for zz in range(4):
+        for zz in (0, 2, 1, 3):
             (self.xcopy if zz < 2 else self.ycopy)(k, p5, bufs, zz).start()
+
+    def twos(self, k, p5, bufs):
+        for zz in (0, 2, 1, 3):
+            self.two(k, p5, bufs, zz)
+
+    def threes(self, k, p5, bufs):
+        for i in (1, 2, 3):
+            self.three(k, p5, bufs, i)
 
     def two(self, k, p5, bufs, zz):
         col = self.pc.ny if zz < 2 else self.pc.nx
@@ -849,6 +977,7 @@
     nrm, val, gm, gn, hid, slo, atl, atm, ats, gsl, gsm, gd, wv, lv, dwf, vsb, vv, own,
     pd, pll, pv, ad, xd, yd, zd, al, xl, yl, zl, av, xv, yv, zv, std, stl, stv,
     as_, ar, xs, xr, ys, yr, zs, zr, os_, or_, lsem, ssem, rsem, gs_, gr_, free, hsem, fsem, dsem,
+    fss, fsr,
 ):
     pc = Place()
     c = pc.c
@@ -870,14 +999,16 @@
     slo_load = lambda h, b: copy(slo_i.at[h, pl.ds(b * 512, 512)], slo.at[b % 2], hsem.at[6 + b % 2])
     for cp in att_loads(0) + [hid_load(0), l_load(0), slo_load(0, 0), slo_load(0, 1), w_load(0)]:
         cp.start()
-    own_load = lambda f, zz: copy(def_in.at[c, f, zz], own.at[zz % 2], fsem.at[zz % 2])
-    own_load(0, 0).start()
-    own_load(0, 1).start()
+    order = [(f, zz) for f in (1, 0) for zz in (0, 2, 1, 3)]
+    own_load = lambda i: copy(def_in.at[(c,) + order[i]], own.at[i % 2], fsem.at[i % 2])
+    own_load(0).start()
+    own_load(1).start()
 
     greet(pc.near())
-    swaps = []
-    for f in range(2):
-        swaps.append(remote(def_in.at[o, f], pd.at[f], ssem.at[f], rsem.at[f], pc.sib))
+    fswaps = []
+    for i, (f, zz) in enumerate(order):
+        fswaps.append(remote(def_in.at[o, f, zz], pd.at[f, zz], fss.at[i], fsr.at[i], pc.sib))
+    swaps = [None, None]
     swaps.append(remote(do_in.at[o], pv, ssem.at[2], rsem.at[2], pc.sib))
     for i, (at, to) in enumerate(((512, 0), (0, 1024))):
         swaps.append(
@@ -889,8 +1020,8 @@
                 pc.sib,
             )
         )
-    for i in (3, 4, 0, 1, 2):
-        swaps[i].start()
+    for cp in fswaps[0:4] + swaps[3:5] + fswaps[4:8] + swaps[2:3]:
+        cp.start()
 
     def d_args(k):
         slot = k % 3
@@ -899,26 +1030,40 @@
     def l_args(p):
         return pll.at[p % 2], (al.at[p], xl.at[p], yl.at[p], zl.at[p])
 
-    v_args = (pv, (av, xv, yv, zv))
+    def v_args(p):
+        return pv.at[p], (av.at[p], xv.at[p], yv.at[p], zv.at[p])
+
     gn[...] = jnp.zeros_like(gn)
     gsm[...] = jnp.zeros_like(gsm)
 
-    for f in range(2):
-        swaps[f].wait()
+
+    def core_sum(i):
+        f, zz = order[i]
+        fswaps[i].wait()
+        own_load(i).wait()
+        pd[f, zz] = (pd[f, zz].astype(f32) + own[i % 2].astype(f32)).astype(bf16)
+        if i < 6:
+            own_load(i + 2).start()
+        s.row(f, *d_args(f), zz)
+
+    dloads = []
+    for r in range(3):
         for zz in range(4):
-            own_load(f, zz).wait()
-            pd[f, zz] = (pd[f, zz].astype(f32) + own[zz % 2].astype(f32)).astype(bf16)
-            if zz < 2:
-                own_load(f, zz + 2).start()
-            elif f == 0:
-                own_load(1, zz - 2).start()
-        s.one(f, *d_args(f))
-    dloads = []
-    for zz in range(4):
-        lanes = pl.ds(HALF * (zz % 2), HALF)
-        dloads.append(copy(do_in.at[c, zz], own.at[zz // 2, :, :, :, lanes], dsem.at[zz]))
-    for cp in dloads:
-        cp.start()
+            to = pl.ds(HALF * (zz % 2) + 128 * r, 128)
+            dloads.append(copy(do_in.at[c, r, zz], own.at[zz // 2, :, :, :, to], dsem.at[r, zz]))
+
+    def other_half():
+        for i in range(4, 8):
+            core_sum(i)
+        for cp in dloads:
+            cp.start()
+
+    def dloads_done():
+        for cp in swaps[2:3] + dloads:
+            cp.wait()
+
+    for i in range(4):
+        core_sum(i)
     swaps[3].wait()
     swaps[4].wait()
     for cp in first:
@@ -955,27 +1100,31 @@
         dslot = kd % 3
 
         def on_a(fn):
+            fn(kd - 1, *d_args(kd - 1))
+
+        def on_b(fn):
             @pl.when(begin)
             def _():
                 fn(0, *d_args(0))
 
             @pl.when(later)
             def _():
-                fn(kd - 1, *d_args(kd - 1))
-
-        def on_b(fn):
-            @pl.when(begin)
-            def _():
-                fn(1, *d_args(1))
-
+                fn(5 + (p + 2) % 3, *l_args((p + 2) % 3))
+
+        def on_first(*fns):
+            for r, fn in enumerate(fns):
+                if fn is not None:
+                    pl.when(p == r)(fn)
+
+        def on_v(fn):
             @pl.when(later)
             def _():
-                fn(5 + (p + 2) % 3, *l_args((p + 2) % 3))
+                fn(8 + (p + 2) % 3, *v_args((p + 2) % 3))
 
         def four_a():
             @pl.when(begin)
             def _():
-                s.four(0, *d_args(0), std.at[0], ofe.at[c, 0])
+                s.four(1, *d_args(1), std.at[1], ofe.at[c, 1])
 
             @pl.when(p == 2)
             def _():
@@ -989,12 +1138,79 @@
         def four_b():
             @pl.when(begin)
             def _():
-                s.four(1, *d_args(1), std.at[1], ofe.at[c, 1])
+                s.four(0, *d_args(0), std.at[0], ofe.at[c, 0])
 
             @pl.when(later)
             def _():
                 r = (p + 2) % 3
                 s.four(5 + r, *l_args(r), stl.at[r], ol.at[3 * c + r])
+
+        def four_v():
+            @pl.when(later)
+            def _():
+                r = (p + 2) % 3
+                s.four(8 + r, *v_args(r), stv.at[r], ovo.at[r, c])
+
+        def value_part():
+            for half in range(2):
+                cols = slice(half * HALF, half * HALF + HALF)
+                dwf[:, 0:128] = dot(nrm[:, cols], gm[:, lanes], TN)
+
+                @pl.loop(0, 8)
+                def _(i):
+                    for zi in range(2):
+                        row = pl.ds(pl.multiple_of(zi * 192 + i * 24, 8), 24)
+                        at = (2 * half + zi, i // 4, i % 4)
+                        to = pl.ds(pl.multiple_of(HALF * zi + 128 * p, 128), 128)
+                        both = pv[(p,) + at].astype(f32) + own[half, i // 4, i % 4, :, to].astype(f32)
+                        pv[(p,) + at] = jnp.concatenate([dwf[row, 0:128], both[24:48]], axis=0).astype(bf16)
+
+        def tick(e, what):
+            if what == "gs" and e == 0:
+                on_first(lambda: s.twos(1, *d_args(1)))
+                on_v(s.threes)
+            elif what == "gd" and e == 0:
+                on_first(other_half)
+                four_v()
+            elif what == "dw" and e == 0:
+                on_b(s.twos)
+            elif what == "gs":
+                on_first(dloads_done)
+                value_part()
+                s.one(8 + p, *v_args(p))
+                on_a(s.threes)
+            elif what == "gd":
+                on_b(s.threes)
+            elif what == "dw":
+                s.twos(8 + p, *v_args(p))
+                s.one(kd, *d_args(kd))
+            elif what == "dl" and e == 1:
+                s.one(5 + p, *l_args(p))
+                four_a()
+            elif what == "gn" and e == 1:
+                s.twos(kd, *d_args(kd))
+                four_b()
+
+        def logit_part(e):
+            h = 2 * p + e
+            if e == 0:
+
+                @pl.when(p == 2)
+                def _():
+                    s.sent(5, *l_args(0))
+
+            hid_load(h).wait()
+            for half in range(2):
+                cols = slice(half * HALF, half * HALF + HALF)
+                dwf[:, 0:512] = dot(hid[0:1024, cols], gsl[e], TN)
+                dwf[:, 0:256] += dot(hid[1024:2048, cols], gsm[e], TN)
+                put_pair(pll.at[p % 2], half, e, 512)
+
+            @pl.when(h < 5)
+            def _():
+                hid_load(h + 1).start()
+
+            tick(e, "dl")
 
         for e in range(2):
             h = 2 * p + e
@@ -1016,7 +1232,7 @@
                 gkeep = gpair * keeps[e]
                 if b < 2:
                     att = atl[rows]
-                    gsl[rows] = score_grad(att, dot(gpair, vpair, NT))
+                    gsl[e, rows] = score_grad(att, dot(gpair, vpair, NT))
                     vs = dot(att, gkeep, TN)
                 else:
                     part = slice((b - 2) * 256, (b - 2) * 256 + 256)
@@ -1025,8 +1241,8 @@
                         [dot(gpair[0:128], vpair[0:128], NT), dot(gpair[128:256], vpair[128:256], NT)], axis=0
                     )
                     at2 = (b - 2) * 512
-                    gsm[at2 : at2 + 256, 0:128] = score_grad(sh, g_sh)
-                    gsm[at2 + 256 : at2 + 512] = score_grad(mi, dot(gpair[256:512], vpair[256:512], NT))
+                    gsm[e, at2 : at2 + 256, 0:128] = score_grad(sh, g_sh)
+                    gsm[e, at2 + 256 : at2 + 512] = score_grad(mi, dot(gpair[256:512], vpair[256:512], NT))
                     vs = jnp.concatenate(
                         [
                             dot(sh[0:128], gkeep[0:128], TN),
@@ -1040,41 +1256,18 @@
                 else:
                     gm[rows, lanes] = vsb[rows] + vs.astype(bf16)
             ahead(*att_loads(h + 1))
-            lsum = dot(ones, gsl[...])
+            lsum = dot(ones, gsl[e])
             lb_o[pl.ds(h, 1)] = lsum[0:1]
-            lb_o[pl.ds(h, 1), 0:256] += dot(ones, gsm[...])[0:1]
-            if e == 0:
-                on_a(lambda k, p5, bufs: s.two(k, p5, bufs, 0))
-                on_a(lambda k, p5, bufs: s.two(k, p5, bufs, 2))
-            else:
-                for i in (1, 2, 3):
-                    on_a(lambda k, p5, bufs, i=i: s.three(k, p5, bufs, i))
-            if e == 0:
-
-                @pl.when(p == 2)
-                def _():
-                    s.sent(5, *l_args(0))
-
-            hid_load(h).wait()
-            for half in range(2):
-                cols = slice(half * HALF, half * HALF + HALF)
-                dwf[:, 0:512] = dot(hid[0:1024, cols], gsl[...], TN)
-                dwf[:, 0:256] += dot(hid[1024:2048, cols], gsm[...], TN)
-                put_pair(pll.at[p % 2], half, e, 512)
-            ahead(hid_load(h + 1))
-            if e == 1:
-                s.one(5 + p, *l_args(p))
-            else:
-                on_a(lambda k, p5, bufs: s.two(k, p5, bufs, 1))
-                on_a(lambda k, p5, bufs: s.two(k, p5, bufs, 3))
+            lb_o[pl.ds(h, 1), 0:256] += dot(ones, gsm[e])[0:1]
+            tick(e, "gs")
             l_load(h).wait()
             for b in range(4):
                 rows = slice(b * 512, b * 512 + 512)
                 slo_load(h, b).wait()
                 if b < 2:
-                    gh = dot(gsl[rows], lv[...], NT)
+                    gh = dot(gsl[e, rows], lv[...], NT)
                 else:
-                    gh = dot(gsm[(b - 2) * 512 : (b - 2) * 512 + 512], lv[:, 0:256], NT)
+                    gh = dot(gsm[e, (b - 2) * 512 : (b - 2) * 512 + 512], lv[:, 0:256], NT)
                 gd[rows] = (gh * slo[b % 2].astype(f32)).astype(bf16)
                 if b < 2:
                     slo_load(h, b + 2).start()
@@ -1082,12 +1275,7 @@
                     ahead(slo_load(h + 1, b - 2))
             ahead(l_load(h + 1))
             db_o[pl.ds(h, 1)] = (dot(ones, gd[0:1024]) + dot(ones, gd[1024:2048]))[0:1]
-            if e == 0:
-                on_b(lambda k, p5, bufs: s.two(k, p5, bufs, 0))
-                on_b(lambda k, p5, bufs: s.two(k, p5, bufs, 2))
-            else:
-                for i in (1, 2, 3):
-                    on_b(lambda k, p5, bufs, i=i: s.three(k, p5, bufs, i))
+            tick(e, "gd")
             if e == 0:
 
                 @pl.when(later)
@@ -1098,12 +1286,10 @@
                 cols = slice(half * HALF, half * HALF + HALF)
                 dwf[...] = dot(nrm[:, cols], gd[...], TN)
                 put_pair(pd.at[dslot], half, e, D)
+            tick(e, "dw")
             if e == 1:
-                s.one(kd, *d_args(kd))
-                four_a()
-            else:
-                on_b(lambda k, p5, bufs: s.two(k, p5, bufs, 1))
-                on_b(lambda k, p5, bufs: s.two(k, p5, bufs, 3))
+                logit_part(0)
+                logit_part(1)
             w_load(h).wait()
 
             @pl.loop(0, 4)
@@ -1112,46 +1298,17 @@
                 gn[rows] += dot(gd[rows], wv[...], NT)
 
             ahead(w_load(h + 1))
-            if e == 1:
-                four_b()
-
+            tick(e, "gn")
+
+    pl.semaphore_signal(free, inc=1, device_id=pc.sib, device_id_type=MESH)
     vb_o[...] = dot(ones, gm[0:1024]) + dot(ones, gm[1024:2048])
-    swaps[2].wait()
-    for cp in dloads:
-        cp.wait()
-    for half in range(2):
-        cols = slice(half * HALF, half * HALF + HALF)
-        dwf[:, 0:HALF] = dot(nrm[:, cols], gm[...], TN)
-
-        for zi in range(2):
-
-            @pl.loop(0, 8)
-            def _(i):
-                row = pl.ds(pl.multiple_of(zi * 192 + i * 24, 8), 24)
-                part = dwf[row, 0:HALF]
-                at = (2 * half + zi, i // 4, i % 4)
-                mine = own[half, i // 4, i % 4, :, HALF * zi : HALF * zi + HALF]
-                both = pv[at].astype(f32) + mine.astype(f32)
-                pv[at] = jnp.concatenate([part, both[24:48]], axis=0).astype(bf16)
-
-    s.one(8, *v_args)
-    for zz in (0, 2):
-        s.two(4, *d_args(4), zz)
-    for zz in (0, 2):
-        s.two(7, *l_args(2), zz)
-    pl.semaphore_signal(free, inc=1, device_id=pc.sib, device_id_type=MESH)
 
     @pl.loop(0, 4)
     def _(b):
         rows = pl.ds(pl.multiple_of(b * 512, 512), 512)
         gn[rows] += dot(gm[rows], vv[...], NT)
 
-    for zz in (1, 3):
-        s.two(4, *d_args(4), zz)
-    for zz in (1, 3):
-        s.two(7, *l_args(2), zz)
-    for zz in (0, 2, 1, 3):
-        s.two(8, *v_args, zz)
+    s.threes(10, *v_args(2))
     other = lambda to: pl.ds(pl.multiple_of(to + o * 512, 512), 512)
     mine = lambda to: pl.ds(pl.multiple_of(to + c * 512, 512), 512)
     hid[0:512] = gn[other(1024)].astype(bf16)
@@ -1162,10 +1319,7 @@
     tloads = [copy(tok.at[pl.ds(i * 512, 512)], slo.at[i], hsem.at[6 + i]) for i in range(2)]
     for cp in tloads:
         cp.start()
-    for i in (1, 2, 3):
-        s.three(4, *d_args(4), i)
-    for i in (1, 2, 3):
-        s.three(7, *l_args(2), i)
+    s.twos(7, *l_args(2))
     for cp in tloads:
         cp.wait()
     gswap.wait()
@@ -1189,18 +1343,18 @@
         store.start()
         store.wait()
 
-    for i in (1, 2, 3):
-        s.three(8, *v_args, i)
+    s.threes(4, *d_args(4))
+    s.threes(7, *l_args(2))
+    s.four(10, *v_args(2), stv.at[2], ovo.at[2, c])
     for cp in s.outs(1, std.at[1], ofe.at[c, 1]):
         cp.wait()
     s.four(4, *d_args(4), std.at[1], od.at[3 * c + 2])
     s.four(7, *l_args(2), stl.at[2], ol.at[3 * c + 2])
-    s.four(8, *v_args, stv, ovo.at[c])
     ends = []
     for p in range(3):
         ends.append(s.outs(2 + p, std.at[(2 + p) % 3], od.at[3 * c + p]))
         ends.append(s.outs(5 + p, stl.at[p], ol.at[3 * c + p]))
-    ends.append(s.outs(8, stv, ovo.at[c]))
+        ends.append(s.outs(8 + p, stv.at[p], ovo.at[p, c]))
     for pair in ends:
         for cp in pair:
             cp.wait()
@@ -1208,7 +1362,8 @@
         s.sent(k, *d_args(k))
     for p in (1, 2):
         s.sent(5 + p, *l_args(p))
-    s.sent(8, *v_args)
+    for p in range(3):
+        s.sent(8 + p, *v_args(p))
 
 
 def k3_call(*args):
@@ -1226,7 +1381,7 @@
             sds((6, 48, D), f32),
             sds((6, 48, L3), f32),
             sds((2, 2, 48, D), f32),
-            sds((2, 48, HALF), f32),
+            sds((3, 2, 48, 128), f32),
             sds((8, D), f32),
             sds((8, L3), f32),
             sds((8, HALF), f32),
@@ -1244,8 +1399,8 @@
             V((1024, L3), bf16),
             V((512, L2), bf16),
             V((512, L1), bf16),
-            V((1024, L3), bf16),
-            V((1024, L2), bf16),
+            V((2, 1024, L3), bf16),
+            V((2, 1024, L2), bf16),
             V((CHIP_ROWS, HIDDEN_SIZE), bf16),
             V((D, HIDDEN_SIZE), bf16),
             V((HIDDEN_SIZE, L3), bf16),
@@ -1255,15 +1410,16 @@
             V((2, 2, 4, 48, D), bf16),
             V((3, 4, 2, 4, 48, D), bf16),
             V((2, 4, 2, 4, 48, L3), bf16),
-            V((4, 2, 4, 48, HALF), bf16),
+            V((3, 4, 2, 4, 48, 128), bf16),
         ]
         + bufs((5,), D)
         + bufs((3,), L3)
-        + bufs((), HALF)
-        + [V((3, 2, 48, D), f32), V((3, 2, 48, L3), f32), V((2, 48, HALF), f32)]
-        + [dma((9, 4))] * 8
-        + [dma((9, 2)), dma((9,)), dma((8,)), dma((5,)), dma((5,)), dma, dma, pltpu.SemaphoreType.REGULAR]
-        + [dma((8,)), dma((2,)), dma((4,))],
+        + bufs((3,), 128)
+        + [V((3, 2, 48, D), f32), V((3, 2, 48, L3), f32), V((3, 2, 48, 128), f32)]
+        + [dma((11, 4))] * 8
+        + [dma((11, 2)), dma((11,)), dma((8,)), dma((5,)), dma((5,)), dma, dma, pltpu.SemaphoreType.REGULAR]
+        + [dma((8,)), dma((2,)), dma((3, 4))]
+        + [dma((8,))] * 2,
         compiler_params=pltpu.CompilerParams(
             collective_id=2, has_side_effects=True, vmem_limit_bytes=VMEM_LIMIT
         ),
@@ -1304,11 +1460,11 @@
 def k4_call(g):
     return pl.pallas_call(
         k4_kernel,
-        out_shape=jax.ShapeDtypeStruct((8, 128), f32),
+        out_shape=jax.ShapeDtypeStruct((16, 128), f32),
         in_specs=[VMEM],
         out_specs=VMEM,
         scratch_shapes=[
-            pltpu.VMEM((32, 8, 128), f32),
+            pltpu.VMEM((32, 16, 128), f32),
             pltpu.SemaphoreType.DMA((32,)),
             pltpu.SemaphoreType.DMA((32,)),
         ],
@@ -1332,35 +1488,33 @@
     lb_all = lax.dynamic_update_slice(jnp.zeros((HEADS, L3), f32), lbs[0:6], (6 * core, 0))
     db_all = lax.dynamic_update_slice(jnp.zeros((HEADS, HIDDEN_SIZE), f32), dbs[0:6], (6 * core, 0))
     v7 = jnp.concatenate([ags[0:2], vb_all, sums[3:4], sums[0:2], sums[2:3]])
+    narrow_rows = v7.reshape(7, 32, 24).transpose(1, 0, 2)
+    wide_rows = jnp.concatenate(
+        [sums[4:8].reshape(32, 1, 96), lb_all.reshape(32, 2, 96), db_all.reshape(32, 3, 96)], axis=1
+    )
     pack = jnp.concatenate(
-        [
-            v7.reshape(7, 32, 24).transpose(1, 0, 2).reshape(32, 168),
-            sums[4:8].reshape(32, 96),
-            lb_all.reshape(32, 192),
-            db_all.reshape(32, 288),
-            jnp.zeros((32, 1024 - 744), f32),
-        ],
-        axis=1,
-    )
-    red = k4_call(pack.reshape(32, 8, 128)).reshape(1024)
-    small = lambda i: red[24 * i : 24 * i + 24]
+        [jnp.pad(narrow_rows, ((0, 0), (0, 0), (0, 104))), jnp.pad(wide_rows, ((0, 0), (0, 3), (0, 32)))], axis=1
+    )
+    red = k4_call(pack)
+    vo_shard = lambda r: dvo[:, :, r : r + 24].transpose(2, 1, 0, 3).reshape(24, D)
+    small = lambda i: red[i, :24]
     return (
         lay,
         tg,
         small(0),
         small(1),
         od.reshape(HEADS, 24, HIDDEN_SIZE),
-        red[456:744],
+        red[10:13, :96].reshape(288),
         ol.reshape(HEADS, 24, L3),
-        red[264:456],
-        dvo[:, 0:24].transpose(1, 0, 2).reshape(24, D),
+        red[8:10, :96].reshape(192),
+        vo_shard(0),
         small(2),
-        dvo[:, 24:48].transpose(1, 0, 2).reshape(24, D),
+        vo_shard(24),
         small(3),
         small(4),
         small(5),
         ofe[0].reshape(4, 24, D).transpose(1, 0, 2).reshape(24, 4 * D),
-        red[168:264],
+        red[7, :96],
         ofe[1].reshape(96, D),
         small(6),
     )

time: 509 us -> 480 us (0.943)
  Pallas kernels: 466 us -> 441 us
  local copies, waits for them, and re-layouts: 35 us -> 28.3 us
    pallas_call x1, Pallas kernels: 185 us -> 164 us  [k1_call(): pl.pallas_call(k1_kernel, out_shape=(sds((2, 4, 2, 4, 48, HALF), bf16), s...]
    concatenate x2 -> x0, local copies, waits for them, and re-layouts: 8.25 us -> none  [the longest x1 7.37 us: prepare(): jnp.concatenate([attn_gain, attn_shift, value_bias, output_bias, feed_gai...]
where the time goes in v1:
time: 480 us; the launch traced here: 476 us
  Pallas kernels  441 us (92%)
  local copies, waits for them, and re-layouts  28.3 us (6%)
    pallas_call x1, Pallas kernels, k3_call(): pl.pallas_call(k3_kernel, out_shape=(sds((ROWS_DEV, D), f32), sds((6, 48,...  195 us
    pallas_call x1, Pallas kernels, k1_call(): pl.pallas_call(k1_kernel, out_shape=(sds((2, 4, 2, 4, 48, HALF), bf16), s...  164 us
    pallas_call x1, Pallas kernels, k2_call(): pl.pallas_call(k2_kernel, out_shape=(sds((ROWS_DEV, D), f32), sds((ROWS_D...  55.9 us
    pallas_call x1, Pallas kernels, k0_call(): pl.pallas_call(k0_kernel, out_shape=(sds((32, 16, 128), bf16), sds((ROWS_...  14.7 us
    pallas_call x1, Pallas kernels, k4_call(): pl.pallas_call(k4_kernel, out_shape=jax.ShapeDtypeStruct((16, 128), f32),...  11.7 us

profile of v1, /device:TPU:0, one launch (start us, length us, event | category | flops | bytes accessed | tf_op | source)
XLA Modules:
  0.0 475.7 jit_solution(1349482572604061185)
XLA Ops:
  0.7 0.9 copy.54
  1.6 1.7 pad_maximum_fusion.ff
  3.3 0.8 stack_reshape.12
  4.0 0.8 stack_reshape.13
  5.5 0.8 stack.37
  6.3 0.8 reshape.102
  9.0 14.7 %k0_exchange.1 = (bf16[32,16,128]{2,1,0:T(8,128)(2,1)}, bf16[1024,768]{1,0:T(8,128)(2,1)}, bf16[3,2,48,768]{3,2,1,0:T(8,128)(2,1)}, bf16[3,2,48,512]{3,2,1,0:T(8...) custom-call(bf16[16,128]{1,0:T(8,128)(2,1)} %pad.36.s_in, bf16[1024,768]{1,0:T(8,128)(2,1)} %tok.3, ...), custom_call_target="tpu_custom_call" | custom-call | tf_op jit(solution)/shard_map/k0_exchange/pallas_call | solution.py:145
  23.8 0.9 convert_element_type.19
  25.4 0.9 slice.111
  27.0 0.8 slice.112
  29.3 163.8 %k1_attention.1 = (bf16[2,4,2,4,48,384]{5,4,3,2,1,0:T(8,128)(2,1)}, bf16[3,4,2,4,48,768]{5,4,3,2,1,0:T(8,128)(2,1)}, bf16[3,4,2,4,48,512]{5,4,3,2,1,0:T(8,128)(2...) custom-call(bf16[1024,768]{1,0:T(8,128)(2,1)} %tok.3, ...), custom_call_target="tpu_custom_call" | custom-call | tf_op jit(solution)/shard_map/k1_attention/pallas_call | solution.py:652
  193.9 55.9 %k2_feed.1 = (f32[1024,768]{1,0:T(8,128)}, f32[1024,768]{1,0:T(8,128)}, bf16[2,1024,384]{2,1,0:T(8,128)(2,1)}, bf16[2,2,4,2,4,48,768]{6,5,4,3,2,1,0:T(8,128)(2,1...) custom-call(bf16[1024,768]{1,0:T(8,128)(2,1)} %tok.3, bf16[1024,768]{1,0:T(8,128)(2,1)} %cot.1, ...), custom_call_target="tpu_custom_call" | custom-call | tf_op jit(solution)/shard_map/k2_feed/pallas_call | solution.py:862
  249.8 195.1 %k3_backward.1 = (f32[1024,768]{1,0:T(8,128)}, f32[6,48,768]{2,1,0:T(8,128)}, f32[6,48,512]{2,1,0:T(8,128)}, f32[2,2,48,768]{3,2,1,0:T(8,128)}, f32[3,2,48,128]{...) custom-call(bf16[2,2,4,2,4,48,768]{6,5,4,3,2,1,0:T(8,128)(2,1)} %get-tuple-element., ...), custom_call_target="tpu_custom_call" | custom-call | tf_op jit(solution)/shard_map/k3_backward/pallas_call | solution.py:1377
  445.0 1.0 dynamic_update_slice.11
  446.2 0.9 dynamic_update_slice.10
  449.1 0.7 select_maximum_fusion.2.g
  449.8 11.7 %k4_vectors.1 = f32[16,128]{1,0:T(8,128)} custom-call(f32[32,16,128]{2,1,0:T(8,128)} %select_maximum_fusion.2.g), custom_call_target="tpu_custom_call" | custom-call | tf_op jit(solution)/shard_map/k4_vectors/pallas_call | solution.py:1461
  462.9 1.5 slice_bitcast_fusion.3
  465.6 1.2 slice_bitcast_fusion.4
  466.8 1.8 fusion.9
  469.3 0.9 slice_bitcast_fusion.1
  471.7 1.7 copy.62
  473.5 0.9 copy.63
  474.4 0.8 copy.64
  (51 shorter events, 13.3 us)
Async XLA Ops:
  249.8 197.3 %copy-start.3 = (f32[8,768]{1,0:T(8,128)S(1)}, f32[8,768]{1,0:T(8,128)}, u32[]{:S(2)}) copy-start(f32[8,768]{1,0:T(8,128)} %get-tuple-element.79) | copy-start | bytes 73732
  445.0 26.7 %copy-start = (f32[1024,768]{1,0:T(8,128)S(1)}, f32[1024,768]{1,0:T(8,128)}, u32[]{:S(2)}) copy-start(f32[1024,768]{1,0:T(8,128)} %get-tuple-element.116) | copy-start | bytes 9437188
  471.7 1.8 copy-start.1
  471.7 2.7 copy-start.2

commit v2 on v1

--- a/solution.py
+++ b/solution.py
@@ -94,75 +94,39 @@
     )
 
 
-def k0_kernel(s_in, tok_in, dense, logit, vo, ff, s_all, tok, md, ml, mvo, mf, ss, sr, es, er):
-    pc = Place()
-    c = pc.c
-    me = pc.w * 4 + pc.n
-    bar = pltpu.get_barrier_semaphore()
-
+def everyone(me, fn):
     @pl.loop(1, 32)
     def _(j):
         t = (me + j) % 32
-        pl.semaphore_signal(bar, inc=1, device_id=(t // 4, t % 4), device_id_type=MESH)
-
-    pl.semaphore_wait(bar, 31)
-    o = 1 - c
-
-    @pl.loop(1, 32)
-    def _(j):
-        t = (me + j) % 32
-        remote(s_in, s_all.at[me], ss.at[t], sr.at[me], (t // 4, t % 4)).start()
-
-    pairs = [
-        (dense.at[pl.ds(3 * o, 3)], md.at[:, c]),
-        (logit.at[pl.ds(3 * o, 3)], ml.at[:, c]),
-        (vo.at[o], mvo.at[c]),
-        (ff.at[o], mf.at[:, c]),
-        (tok_in, tok),
-    ]
-    rems = [remote(give, slot, es.at[i], er.at[i], pc.sib) for i, (give, slot) in enumerate(pairs)]
-    for cp in rems:
-        cp.start()
-    s_all[me] = s_in[...]
-    md[:, c] = dense[pl.ds(3 * c, 3)]
-    ml[:, c] = logit[pl.ds(3 * c, 3)]
-    mvo[c] = vo[c]
-    mf[:, c] = ff[c]
-    for cp in rems:
-        cp.wait()
-
-    @pl.loop(1, 32)
-    def _(j):
-        t = (me + j) % 32
-        f = (me + 32 - j) % 32
-        cp = remote(s_in, s_all.at[f], ss.at[t], sr.at[f], (t // 4, t % 4))
-        cp.wait_send()
-        cp.wait_recv()
-
-
-def k0_call(s_in, tok, dense, logit, vo, ff):
-    sds = jax.ShapeDtypeStruct
-    return pl.pallas_call(
-        k0_kernel,
-        out_shape=(
-            sds((32, 16, 128), bf16),
-            sds((ROWS_DEV, D), bf16),
-            sds((3, 2, 48, D), bf16),
-            sds((3, 2, 48, L3), bf16),
-            sds((2, 48, HALF), bf16),
-            sds((2, 2, 48, D), bf16),
-        ),
-        in_specs=[VMEM, HBM, VMEM, VMEM, VMEM, VMEM],
-        out_specs=(VMEM, HBM, VMEM, VMEM, VMEM, VMEM),
-        scratch_shapes=[
-            pltpu.SemaphoreType.DMA((32,)),
-            pltpu.SemaphoreType.DMA((32,)),
-            pltpu.SemaphoreType.DMA((5,)),
-            pltpu.SemaphoreType.DMA((5,)),
-        ],
-        compiler_params=pltpu.CompilerParams(collective_id=0, has_side_effects=True),
-        name="k0_exchange",
-    )(s_in, tok, dense, logit, vo, ff)
+        fn(t, (me + 32 - j) % 32, (t // 4, t % 4))
+
+
+def spread(s_all, rows, width, count, base):
+    n = len(rows)
+    parts = jnp.concatenate([s_all[:, r, :] for r in rows], axis=0).astype(bf16)
+    q = lax.broadcasted_iota(jnp.int32, (8, 32 * n), 1)
+    h = lax.broadcasted_iota(jnp.int32, (8, 32 * n), 0) + base
+    piece = n * (q & 31) + (q >> 5)
+    lane = lax.broadcasted_iota(jnp.int32, (128, 8 * width), 0)
+    to = lax.broadcasted_iota(jnp.int32, (128, 8 * width), 1)
+    out = jnp.zeros((8, 8 * width), f32)
+    for pos in range(8):
+        pick = jnp.where(piece == 8 * h + pos, 1.0, 0.0).astype(bf16)
+        move = jnp.where((to == width * pos + lane) & (lane < width), 1.0, 0.0).astype(bf16)
+        out = out + dot(dot(pick, parts).astype(bf16), move)
+    return out[0:count]
+
+
+def spread_narrow(s_all, vec):
+    dev = lax.broadcasted_iota(jnp.int32, (32, D), 0)
+    owner = (lax.broadcasted_iota(jnp.int32, (32, D), 1) * 2731) >> 16
+    lane = lax.broadcasted_iota(jnp.int32, (128, D), 0)
+    to = lax.broadcasted_iota(jnp.int32, (128, D), 1)
+    move = jnp.where(to - 24 * ((to * 2731) >> 16) == lane, 1.0, 0.0).astype(bf16)
+    for i in range(7):
+        wide = dot(s_all[:, i, :].astype(bf16), move)
+        vec[i : i + 1] = jnp.sum(jnp.where(owner == dev, wide, 0.0), axis=0, keepdims=True)
+    vec[7:8] = jnp.zeros((1, D), f32)
 
 
 class Gather:
@@ -358,23 +322,47 @@
 
 
 def k1_kernel(
-    tok, tok2, vec, db, lb, vb, mvo, md, ml, mf,
-    ovo, gd, gl, ef, nrm_o, val_o, hid_o, slo_o, atl_o, atm_o, ats_o, wa_o, la_o, mix_o, vv_o,
-    tokv, nrm, val, vst, vv, wst, lst, wv, lv, hidv, slov, atlv, atmv, atsv, mixv,
+    s_in, tok, dense, logit, vo, ff,
+    ovo, gd, gl, ef, nrm_o, val_o, hid_o, slo_o, atl_o, atm_o, ats_o, wa_o, la_o, mix_o, vv_o, vec, eb,
+    s_all, db, lb, vb, mvo, md, ml, mf, tokv, nrm, val, vst, vv, wst, lst, wv, lv, hidv, slov, atlv, atmv, atsv, mixv,
     zs, zr, xs, xr, ys, yr, ds, dr, ls, tsem, osem, wsem, lsem, ssem, rsem, msem,
-    cs, cr, us, ur, vs, vr, cls, ps, pr,
+    cs, cr, us, ur, vs, vr, cls, ps, pr, vss, vsr, es, er,
 ):
     pc = Place()
     c = pc.c
     g = Gather(pc, (zs, zr, xs, xr, ys, yr, ds, dr, ls))
+    o = 1 - c
+    me = pc.w * 4 + pc.n
     tcopies = []
-    for i, (ref, d) in enumerate(((tok, c), (tok2, 1 - c))):
-        for j, (at, to) in enumerate(((512, d * 512), (0, 1024 + d * 512))):
-            rows = pl.ds(pl.multiple_of(to, 512), 512)
-            tcopies.append(pltpu.make_async_copy(ref.at[pl.ds(at, 512)], tokv.at[rows], tsem.at[2 * i + j]))
+    trows = [pl.ds(pl.multiple_of(to + c * 512, 512), 512) for to in (0, 1024)]
+    for i, at in enumerate((512, 0)):
+        tcopies.append(pltpu.make_async_copy(tok.at[pl.ds(at, 512)], tokv.at[trows[i]], tsem.at[i]))
     for cp in tcopies:
         cp.start()
-    greet(pc.near())
+    bar = pltpu.get_barrier_semaphore()
+    everyone(me, lambda t, f, dev: pl.semaphore_signal(bar, inc=1, device_id=dev, device_id_type=MESH))
+    pl.semaphore_wait(bar, 31)
+    gives = [
+        (vo.at[o], mvo.at[c]),
+        (dense.at[pl.ds(3 * o, 3)], md.at[:, c]),
+        (ff.at[o], mf.at[:, c]),
+        (logit.at[pl.ds(3 * o, 3)], ml.at[:, c]),
+    ]
+    for i, at in enumerate((512, 0)):
+        gives.append((tok.at[pl.ds(at, 512)], tokv.at[trows[i]]))
+    rems = [remote(give, slot, es.at[i], er.at[i], pc.sib) for i, (give, slot) in enumerate(gives)]
+    for cp in rems[0:4]:
+        cp.start()
+    everyone(me, lambda t, f, dev: remote(s_in, s_all.at[me], vss.at[t], vsr.at[me], dev).start())
+    mvo[c] = vo[c]
+    md[:, c] = dense[pl.ds(3 * c, 3)]
+    mf[:, c] = ff[c]
+    ml[:, c] = logit[pl.ds(3 * c, 3)]
+    small = lambda t, f, dev: remote(s_in, s_all.at[f], vss.at[t], vsr.at[f], dev)
+    for cp in rems[4:6]:
+        cp.start()
+    for cp in rems[0:4]:
+        cp.wait()
 
     vo_args = (0, mvo, ovo.at[c])
     dd = lambda p: (1 + 2 * p, md.at[p], gd.at[p])
@@ -388,8 +376,26 @@
     g.col(*dd(0), 0)
     fa.first()
     g.col(*ll(0), 0)
-
-    for cp in tcopies:
+    s_all[me] = s_in[...]
+
+    for i in (1, 2, 3):
+        g.col(*vo_args, i)
+    g.zsend(*ll(0))
+    fa.second()
+    g.col(*dd(1), 0)
+
+    def arrived(t, f, dev):
+        small(t, f, dev).wait_send()
+        small(t, f, dev).wait_recv()
+
+    everyone(me, arrived)
+    spread_narrow(s_all, vec)
+    db[0:6] = spread(s_all, (11, 12, 13), 96, 6, 6 * c)
+    lb[0:6] = spread(s_all, (8, 9, 10), 64, 6, 6 * c)
+    eb[...] = spread(s_all, (7,), 96, 4, 0)
+    vb[0:1] = jnp.where(c == 0, vec[2:3, 0:HALF], vec[2:3, HALF:D])
+
+    for cp in tcopies + rems[4:6]:
         cp.wait()
 
     @pl.loop(0, 8)
@@ -400,11 +406,6 @@
 
     nrm_copy = pltpu.make_async_copy(nrm, nrm_o, tsem.at[4])
     nrm_copy.start()
-    for i in (1, 2, 3):
-        g.col(*vo_args, i)
-    g.zsend(*ll(0))
-    fa.second()
-    g.col(*dd(1), 0)
     for i in (1, 2, 3):
         g.col(*dd(0), i)
     g.zsend(*dd(1))
@@ -432,7 +433,7 @@
     @pl.loop(0, 4)
     def _(b):
         rows = pl.ds(pl.multiple_of(b * 512, 512), 512)
-        val[rows] = (dot(nrm[rows], vv[...]) + vb[...]).astype(bf16)
+        val[rows] = (dot(nrm[rows], vv[...]) + vb[0:1]).astype(bf16)
 
     val_copy = pltpu.make_async_copy(val, val_o, tsem.at[6])
     val_copy.start()
@@ -624,7 +625,6 @@
 
     fb_swap = lambda r: remote(ef.at[c, 1, r], ef.at[c, 1, r], ssem.at[4 + r], rsem.at[4 + r], pc.sib)
     swaps = [vo_swap]
-    o = 1 - c
     for i, (start, to) in enumerate(((0, 512), (1024, 0))):
         mine = pltpu.make_async_copy(
             mixv.at[pl.ds(start + c * 512, 512)], mix_o.at[c, pl.ds(to, 512)], msem.at[i]
@@ -646,7 +646,7 @@
     g.sent(*fb)
 
 
-def k1_call(tok, tok2, vec, db, lb, vb, mvo, md, ml, mf):
+def k1_call(s_in, tok, dense, logit, vo, ff):
     sds = jax.ShapeDtypeStruct
     dma = pltpu.SemaphoreType.DMA
     return pl.pallas_call(
@@ -667,10 +667,20 @@
             sds((6, HIDDEN_SIZE, L3), bf16),
             sds((2, ROWS_DEV, HALF), bf16),
             sds((D, HALF), bf16),
+            sds((8, D), f32),
+            sds((4, D), f32),
         ),
-        in_specs=[HBM] * 2 + [VMEM] * 8,
-        out_specs=(HBM,) * 15,
+        in_specs=[VMEM, HBM] + [VMEM] * 4,
+        out_specs=(HBM,) * 15 + (VMEM,) * 2,
         scratch_shapes=[
+            pltpu.VMEM((32, 16, 128), f32),
+            pltpu.VMEM((8, HIDDEN_SIZE), f32),
+            pltpu.VMEM((8, L3), f32),
+            pltpu.VMEM((8, HALF), f32),
+            pltpu.VMEM((2, 48, HALF), bf16),
+            pltpu.VMEM((3, 2, 48, D), bf16),
+            pltpu.VMEM((3, 2, 48, L3), bf16),
+            pltpu.VMEM((2, 2, 48, D), bf16),
             pltpu.VMEM((CHIP_ROWS, D), bf16),
             pltpu.VMEM((CHIP_ROWS, D), bf16),
             pltpu.VMEM((CHIP_ROWS, HALF), bf16),
@@ -690,24 +700,23 @@
         + gather_sems(8)
         + [dma((9,)), dma((2, 5)), dma, dma, dma((8,)), dma((8,)), dma((2,))]
         + [dma((4,))] * 6
-        + [dma, dma((4,)), dma((4,))],
+        + [dma, dma((4,)), dma((4,)), dma((32,)), dma((32,)), dma((6,)), dma((6,))],
         compiler_params=pltpu.CompilerParams(
             collective_id=1, has_side_effects=True, vmem_limit_bytes=VMEM_LIMIT
         ),
         name="k1_attention",
-    )(tok, tok2, vec, db, lb, vb, mvo, md, ml, mf)
+    )(s_in, tok, dense, logit, vo, ff)
 
 
 def prepare(tokens, attn_gain, attn_shift, dense_weight, dense_bias, logit_weight, logit_bias, value_weight,
             value_bias, output_weight, output_bias, feed_gain, feed_shift, expand_weight, expand_bias,
             reduce_weight, reduce_bias):
-    core = lax.axis_index(AXES[0]) % 2
     narrow_rows = jnp.stack([attn_gain, attn_shift, value_bias, output_bias, feed_gain, feed_shift, reduce_bias])
-    wide_rows = [expand_bias.reshape(1, 96), logit_bias.reshape(2, 96), dense_bias.reshape(3, 96)]
+    wide_rows = [(expand_bias.reshape(1, 96), 32), (logit_bias.reshape(3, 64), 64), (dense_bias.reshape(3, 96), 32)]
     small = jnp.concatenate(
-        [jnp.pad(narrow_rows, ((0, 0), (0, 104)))] + [jnp.pad(v, ((0, 0), (0, 32))) for v in wide_rows]
-    )
-    small = jnp.pad(small, ((0, 3), (0, 0)))
+        [jnp.pad(narrow_rows, ((0, 0), (0, 104)))] + [jnp.pad(v, ((0, 0), (0, pad))) for v, pad in wide_rows]
+    )
+    small = jnp.pad(small, ((0, 2), (0, 0))).astype(f32)
     dense = dense_weight.reshape(6, 48, D)
     logit = logit_weight.reshape(6, 48, L3)
     vo = jnp.stack([value_weight.reshape(24, 2, HALF), output_weight.reshape(24, 2, HALF)]).transpose(2, 0, 1, 3)
@@ -715,14 +724,7 @@
     ff = jnp.stack(
         [expand_weight.reshape(24, 4, D).transpose(1, 0, 2).reshape(2, 48, D), reduce_weight.reshape(2, 48, D)]
     )
-    s_all, tok2, md, ml, mvo, mf = k0_call(small, tokens, dense, logit, vo, ff)
-    every = s_all.astype(f32)
-    vec = every[:, 0:7, :24].transpose(1, 0, 2).reshape(7, D)
-    eb = every[:, 7, :96].reshape(4, D)
-    lb = lax.dynamic_slice(every[:, 8:10, :96].reshape(HEADS, L3), (6 * core, 0), (6, L3))
-    db = lax.dynamic_slice(every[:, 10:13, :96].reshape(HEADS, HIDDEN_SIZE), (6 * core, 0), (6, HIDDEN_SIZE))
-    vb = lax.dynamic_slice(vec[2:3], (0, HALF * core), (1, HALF))
-    return tok2, vec, eb, lb, db, vb, md, ml, mvo, mf
+    return small, tokens, dense, logit, vo, ff
 
 
 def k2_kernel(
@@ -1475,11 +1477,7 @@
 
 def chip_body(tokens, cotangent, bucket_counts, *params):
     core = lax.axis_index(AXES[0]) % 2
-    tok2, vec, eb, lb, db, vb, md, ml, mvo, mf = prepare(tokens, *params)
-    vec = jnp.pad(vec, ((0, 1), (0, 0)))
-    ovo, _, _, ef, nrm, val, hid, slo, atl, atm, ats, wa, la, mix, vv = k1_call(
-        tokens, tok2, vec, db, lb, vb, mvo, md, ml, mf
-    )
+    ovo, _, _, ef, nrm, val, hid, slo, atl, atm, ats, wa, la, mix, vv, vec, eb = k1_call(*prepare(tokens, *params))
     lay, gres, gmix, dff, dout, sums = k2_call(tokens, cotangent, bucket_counts, mix, ovo, ef, vec, eb)
     tg, od, ol, ofe, dvo, dbs, lbs, vbs, ags = k3_call(
         dff, dout, nrm, val, gmix, hid, slo, atl, atm, ats, wa, la, vv, tokens, gres, vec

time: 480 us -> 472 us (0.983)
  local copies, waits for them, and re-layouts: 28.3 us -> 22.4 us
    pallas_call x1 -> x0, Pallas kernels: 14.7 us -> none  [k0_call(): pl.pallas_call(k0_kernel, out_shape=(sds((32, 16, 128), bf16), sds((ROWS_...]
    pallas_call x1, Pallas kernels: 164 us -> 177 us  [k1_call(): pl.pallas_call(k1_kernel, out_shape=(sds((2, 4, 2, 4, 48, HALF), bf16), s...]
where the time goes in v2:
time: 472 us; the launch traced here: 467 us
  Pallas kernels  439 us (93%)
  local copies, waits for them, and re-layouts  22.4 us (5%)
    pallas_call x1, Pallas kernels, k3_call(): pl.pallas_call(k3_kernel, out_shape=(sds((ROWS_DEV, D), f32), sds((6, 48,...  194 us
    pallas_call x1, Pallas kernels, k1_call(): pl.pallas_call(k1_kernel, out_shape=(sds((2, 4, 2, 4, 48, HALF), bf16), s...  177 us
    pallas_call x1, Pallas kernels, k2_call(): pl.pallas_call(k2_kernel, out_shape=(sds((ROWS_DEV, D), f32), sds((ROWS_D...  56 us
    pallas_call x1, Pallas kernels, k4_call(): pl.pallas_call(k4_kernel, out_shape=jax.ShapeDtypeStruct((16, 128), f32),...  11.7 us

profile of v2, /device:TPU:0, one launch (start us, length us, event | category | flops | bytes accessed | tf_op | source)
XLA Modules:
  0.0 467.0 jit_solution(11307619209333854461)
XLA Ops:
  0.7 0.9 copy.52
  1.6 1.7 pad_maximum_fusion.ff
  3.2 0.8 stack_reshape.12
  4.0 0.8 stack_reshape.13
  5.5 0.8 stack.37
  6.3 0.7 reshape.91
  7.0 0.8 reshape.92
  9.0 177.0 %k1_attention.1 = (bf16[2,4,2,4,48,384]{5,4,3,2,1,0:T(8,128)(2,1)}, bf16[3,4,2,4,48,768]{5,4,3,2,1,0:T(8,128)(2,1)}, bf16[3,4,2,4,48,512]{5,4,3,2,1,0:T(8,128)(2...) custom-call(f32[16,128]{1,0:T(8,128)} %pad_convert_fusion.s_in, ...), custom_call_target="tpu_custom_call" | custom-call | tf_op jit(solution)/shard_map/k1_attention/pallas_call | solution.py:652
  186.1 56.0 %k2_feed.1 = (f32[1024,768]{1,0:T(8,128)}, f32[1024,768]{1,0:T(8,128)}, bf16[2,1024,384]{2,1,0:T(8,128)(2,1)}, bf16[2,2,4,2,4,48,768]{6,5,4,3,2,1,0:T(8,128)(2,1...) custom-call(bf16[1024,768]{1,0:T(8,128)(2,1)} %tok.3, bf16[1024,768]{1,0:T(8,128)(2,1)} %cot.1, ...), custom_call_target="tpu_custom_call" | custom-call | tf_op jit(solution)/shard_map/k2_feed/pallas_call | solution.py:864
  242.1 194.1 %k3_backward.1 = (f32[1024,768]{1,0:T(8,128)}, f32[6,48,768]{2,1,0:T(8,128)}, f32[6,48,512]{2,1,0:T(8,128)}, f32[2,2,48,768]{3,2,1,0:T(8,128)}, f32[3,2,48,128]{...) custom-call(bf16[2,2,4,2,4,48,768]{6,5,4,3,2,1,0:T(8,128)(2,1)} %get-tuple-element., ...), custom_call_target="tpu_custom_call" | custom-call | tf_op jit(solution)/shard_map/k3_backward/pallas_call | solution.py:1379
  436.2 1.0 dynamic_update_slice.11
  437.4 0.9 dynamic_update_slice.10
  438.6 0.7 slice_dynamic-update-slice_fusion
  439.3 0.7 slice.65
  440.3 0.7 select_maximum_fusion.2.g
  441.0 11.7 %k4_vectors.1 = f32[16,128]{1,0:T(8,128)} custom-call(f32[32,16,128]{2,1,0:T(8,128)} %select_maximum_fusion.2.g), custom_call_target="tpu_custom_call" | custom-call | tf_op jit(solution)/shard_map/k4_vectors/pallas_call | solution.py:1463
  454.1 1.5 slice_bitcast_fusion.2
  456.9 1.2 slice_bitcast_fusion.3
  458.1 1.8 fusion.9
  459.9 0.7 copy.49
  460.6 0.9 slice_bitcast_fusion
  463.0 1.7 copy.60
  464.8 0.9 copy.61
  465.7 0.8 copy.62
  (34 shorter events, 6.8 us)
Async XLA Ops:
  242.1 196.3 %copy-start.3 = (f32[8,768]{1,0:T(8,128)S(1)}, f32[8,768]{1,0:T(8,128)}, u32[]{:S(2)}) copy-start(f32[8,768]{1,0:T(8,128)} %get-tuple-element.71) | copy-start | bytes 73732
  436.2 26.8 %copy-start = (f32[1024,768]{1,0:T(8,128)S(1)}, f32[1024,768]{1,0:T(8,128)}, u32[]{:S(2)}) copy-start(f32[1024,768]{1,0:T(8,128)} %get-tuple-element.108) | copy-start | bytes 9437188
  463.0 1.8 copy-start.1
  463.0 2.7 copy-start.2

commit v3 on v2

--- a/solution.py
+++ b/solution.py
@@ -974,12 +974,13 @@
 
 
 def k3_kernel(
-    def_in, do_in, nrm_i, val_i, gmix, hid_i, slo_i, atl_i, atm_i, ats_i, wa_i, la_i, vv_i, tok, gres, vec,
-    tg_o, od, ol, ofe, ovo, db_o, lb_o, vb_o, ag_o,
+    def_in, do_in, nrm_i, val_i, gmix, hid_i, slo_i, atl_i, atm_i, ats_i, wa_i, la_i, vv_i, tok, gres, vec, sums,
+    tg_o, od, ol, ofe, ovo, va,
+    db_o, lb_o, vb_o, ag_o, vg, vr, vt,
     nrm, val, gm, gn, hid, slo, atl, atm, ats, gsl, gsm, gd, wv, lv, dwf, vsb, vv, own,
     pd, pll, pv, ad, xd, yd, zd, al, xl, yl, zl, av, xv, yv, zv, std, stl, stv,
     as_, ar, xs, xr, ys, yr, zs, zr, os_, or_, lsem, ssem, rsem, gs_, gr_, free, hsem, fsem, dsem,
-    fss, fsr,
+    fss, fsr, v1s, v1r, v2s, v2r,
 ):
     pc = Place()
     c = pc.c
@@ -1006,7 +1007,10 @@
     own_load(0).start()
     own_load(1).start()
 
-    greet(pc.near())
+    me = pc.w * 4 + pc.n
+    bar = pltpu.get_barrier_semaphore()
+    everyone(me, lambda t, f, dev: pl.semaphore_signal(bar, inc=1, device_id=dev, device_id_type=MESH))
+    pl.semaphore_wait(bar, 31)
     fswaps = []
     for i, (f, zz) in enumerate(order):
         fswaps.append(remote(def_in.at[o, f, zz], pd.at[f, zz], fss.at[i], fsr.at[i], pc.sib))
@@ -1345,13 +1349,47 @@
         store.start()
         store.wait()
 
+    vg[...] = jnp.zeros_like(vg)
+    whole = [ag_o[0:1], ag_o[1:2], None, sums[3:4], sums[0:1], sums[1:2], sums[2:3]]
+    whole += [sums[4 + j : 5 + j] for j in range(4)]
+    for i, row in enumerate(whole):
+        if row is not None:
+            for b in range(6):
+                vg[i, b : b + 1] = row[:, 128 * b : 128 * b + 128]
+    for b in range(3):
+        vg[2, pl.ds(3 * c + b, 1)] = vb_o[0:1, 128 * b : 128 * b + 128]
+    for h in range(6):
+        for b in range(6):
+            vg[11 + 6 * c + h, b : b + 1] = db_o[h : h + 1, 128 * b : 128 * b + 128]
+        for b in range(4):
+            k = 4 * h + b
+            vg[23 + 4 * c + k // 6, k % 6 : k % 6 + 1] = lb_o[h : h + 1, 128 * b : 128 * b + 128]
+    everyone(me, lambda t, f, dev: remote(vg.at[t], vr.at[me], v1s.at[t], v1r.at[me], dev).start())
+    vr[me] = vg[me]
     s.threes(4, *d_args(4))
     s.threes(7, *l_args(2))
+
+    def part_done(t, f, dev):
+        cp = remote(vg.at[t], vr.at[f], v1s.at[t], v1r.at[f], dev)
+        cp.wait_send()
+        cp.wait_recv()
+
+    everyone(me, part_done)
+    vt[...] = jnp.sum(vr[...], axis=0)
+    everyone(me, lambda t, f, dev: remote(vt, va.at[me], v2s.at[t], v2r.at[me], dev).start())
+    va[me] = vt[...]
     s.four(10, *v_args(2), stv.at[2], ovo.at[2, c])
     for cp in s.outs(1, std.at[1], ofe.at[c, 1]):
         cp.wait()
     s.four(4, *d_args(4), std.at[1], od.at[3 * c + 2])
     s.four(7, *l_args(2), stl.at[2], ol.at[3 * c + 2])
+
+    def whole_done(t, f, dev):
+        cp = remote(vt, va.at[f], v2s.at[t], v2r.at[f], dev)
+        cp.wait_send()
+        cp.wait_recv()
+
+    everyone(me, whole_done)
     ends = []
     for p in range(3):
         ends.append(s.outs(2 + p, std.at[(2 + p) % 3], od.at[3 * c + p]))
@@ -1384,14 +1422,18 @@
             sds((6, 48, L3), f32),
             sds((2, 2, 48, D), f32),
             sds((3, 2, 48, 128), f32),
-            sds((8, D), f32),
-            sds((8, L3), f32),
-            sds((8, HALF), f32),
-            sds((8, D), f32),
+            sds((32, 8, 128), f32),
         ),
-        in_specs=[HBM] * 15 + [VMEM],
-        out_specs=(HBM,) * 5 + (VMEM,) * 4,
+        in_specs=[HBM] * 15 + [VMEM] * 2,
+        out_specs=(HBM,) * 5 + (VMEM,),
         scratch_shapes=[
+            V((8, D), f32),
+            V((8, L3), f32),
+            V((8, HALF), f32),
+            V((8, D), f32),
+            V((32, 8, 128), f32),
+            V((32, 8, 128), f32),
+            V((8, 128), f32),
             V((CHIP_ROWS, D), bf16),
             V((CHIP_ROWS, HALF), bf16),
             V((CHIP_ROWS, HALF), bf16),
@@ -1421,7 +1463,8 @@
         + [dma((11, 4))] * 8
         + [dma((11, 2)), dma((11,)), dma((8,)), dma((5,)), dma((5,)), dma, dma, pltpu.SemaphoreType.REGULAR]
         + [dma((8,)), dma((2,)), dma((3, 4))]
-        + [dma((8,))] * 2,
+        + [dma((8,))] * 2
+        + [dma((32,))] * 4,
         compiler_params=pltpu.CompilerParams(
             collective_id=2, has_side_effects=True, vmem_limit_bytes=VMEM_LIMIT
         ),
@@ -1429,82 +1472,27 @@
     )(*args)
 
 
-def k4_kernel(g, out, slots, ss, sr):
-    pc = Place()
-    me = pc.w * 4 + pc.n
-    bar = pltpu.get_barrier_semaphore()
-
-    @pl.loop(1, 32)
-    def _(j):
-        t = (me + j) % 32
-        pl.semaphore_signal(bar, inc=1, device_id=(t // 4, t % 4), device_id_type=MESH)
-
-    pl.semaphore_wait(bar, 31)
-
-    @pl.loop(1, 32)
-    def _(j):
-        t = (me + j) % 32
-        remote(g.at[t], slots.at[me], ss.at[t], sr.at[me], (t // 4, t % 4)).start()
-
-    slots[me] = g[me]
-
-    @pl.loop(1, 32)
-    def _(j):
-        t = (me + j) % 32
-        f = (me + 32 - j) % 32
-        cp = remote(g.at[t], slots.at[f], ss.at[t], sr.at[f], (t // 4, t % 4))
-        cp.wait_send()
-        cp.wait_recv()
-
-    out[...] = jnp.sum(slots[...], axis=0)
-
-
-def k4_call(g):
-    return pl.pallas_call(
-        k4_kernel,
-        out_shape=jax.ShapeDtypeStruct((16, 128), f32),
-        in_specs=[VMEM],
-        out_specs=VMEM,
-        scratch_shapes=[
-            pltpu.VMEM((32, 16, 128), f32),
-            pltpu.SemaphoreType.DMA((32,)),
-            pltpu.SemaphoreType.DMA((32,)),
-        ],
-        compiler_params=pltpu.CompilerParams(collective_id=3, has_side_effects=True),
-        name="k4_vectors",
-    )(g)
-
-
 def chip_body(tokens, cotangent, bucket_counts, *params):
-    core = lax.axis_index(AXES[0]) % 2
     ovo, _, _, ef, nrm, val, hid, slo, atl, atm, ats, wa, la, mix, vv, vec, eb = k1_call(*prepare(tokens, *params))
     lay, gres, gmix, dff, dout, sums = k2_call(tokens, cotangent, bucket_counts, mix, ovo, ef, vec, eb)
-    tg, od, ol, ofe, dvo, dbs, lbs, vbs, ags = k3_call(
-        dff, dout, nrm, val, gmix, hid, slo, atl, atm, ats, wa, la, vv, tokens, gres, vec
-    )
-    vb_all = lax.dynamic_update_slice(jnp.zeros((1, D), f32), vbs[0:1], (0, HALF * core))
-    lb_all = lax.dynamic_update_slice(jnp.zeros((HEADS, L3), f32), lbs[0:6], (6 * core, 0))
-    db_all = lax.dynamic_update_slice(jnp.zeros((HEADS, HIDDEN_SIZE), f32), dbs[0:6], (6 * core, 0))
-    v7 = jnp.concatenate([ags[0:2], vb_all, sums[3:4], sums[0:2], sums[2:3]])
-    narrow_rows = v7.reshape(7, 32, 24).transpose(1, 0, 2)
-    wide_rows = jnp.concatenate(
-        [sums[4:8].reshape(32, 1, 96), lb_all.reshape(32, 2, 96), db_all.reshape(32, 3, 96)], axis=1
-    )
-    pack = jnp.concatenate(
-        [jnp.pad(narrow_rows, ((0, 0), (0, 0), (0, 104))), jnp.pad(wide_rows, ((0, 0), (0, 3), (0, 32)))], axis=1
-    )
-    red = k4_call(pack)
+    tg, od, ol, ofe, dvo, every = k3_call(
+        dff, dout, nrm, val, gmix, hid, slo, atl, atm, ats, wa, la, vv, tokens, gres, vec, sums
+    )
+    me = lax.axis_index(AXES[0]) * 4 + lax.axis_index(AXES[1])
+    every = every[:, :6]
+    v7 = lax.dynamic_slice(every[0:7].reshape(7, D), (0, 24 * me), (7, 24))
+    own = lambda i, j, size: lax.dynamic_slice(every[i:j].reshape(-1), (size * me,), (size,))
     vo_shard = lambda r: dvo[:, :, r : r + 24].transpose(2, 1, 0, 3).reshape(24, D)
-    small = lambda i: red[i, :24]
+    small = lambda i: v7[i]
     return (
         lay,
         tg,
         small(0),
         small(1),
         od.reshape(HEADS, 24, HIDDEN_SIZE),
-        red[10:13, :96].reshape(288),
+        own(11, 23, 288),
         ol.reshape(HEADS, 24, L3),
-        red[8:10, :96].reshape(192),
+        own(23, 31, 192),
         vo_shard(0),
         small(2),
         vo_shard(24),
@@ -1512,7 +1500,7 @@
         small(4),
         small(5),
         ofe[0].reshape(4, 24, D).transpose(1, 0, 2).reshape(24, 4 * D),
-        red[7, :96],
+        own(7, 11, 96),
         ofe[1].reshape(96, D),
         small(6),
     )

time: 472 us -> 462 us (0.979)
  Pallas kernels: 439 us -> 434 us
    pallas_call x1 -> x0, Pallas kernels: 11.7 us -> none  [k4_call(): pl.pallas_call(k4_kernel, out_shape=jax.ShapeDtypeStruct((16, 128), f32),...]
    pallas_call x1, Pallas kernels: 194 us -> 201 us  [k3_call(): pl.pallas_call(k3_kernel, out_shape=(sds((ROWS_DEV, D), f32), sds((6, 48,...]
where the time goes in v3:
time: 462 us; the launch traced here: 458 us
  Pallas kernels  434 us (94%)
  local copies, waits for them, and re-layouts  18.9 us (4%)
    pallas_call x1, Pallas kernels, k3_call(): pl.pallas_call(k3_kernel, out_shape=(sds((ROWS_DEV, D), f32), sds((6, 48,...  201 us
    pallas_call x1, Pallas kernels, k1_call(): pl.pallas_call(k1_kernel, out_shape=(sds((2, 4, 2, 4, 48, HALF), bf16), s...  177 us
    pallas_call x1, Pallas kernels, k2_call(): pl.pallas_call(k2_kernel, out_shape=(sds((ROWS_DEV, D), f32), sds((ROWS_D...  56 us

profile of v3, /device:TPU:0, one launch (start us, length us, event | category | flops | bytes accessed | tf_op | source)
XLA Modules:
  0.0 457.7 jit_solution(18135915578341686194)
XLA Ops:
  0.7 0.9 copy.52
  1.6 1.7 pad_maximum_fusion.ff
  3.2 0.8 stack_reshape.12
  4.0 0.8 stack_reshape.13
  5.5 0.8 stack.37
  6.3 0.7 reshape.85
  7.0 0.8 reshape.86
  7.8 0.7 fusion.7
  9.0 177.0 %k1_attention.1 = (bf16[2,4,2,4,48,384]{5,4,3,2,1,0:T(8,128)(2,1)}, bf16[3,4,2,4,48,768]{5,4,3,2,1,0:T(8,128)(2,1)}, bf16[3,4,2,4,48,512]{5,4,3,2,1,0:T(8,128)(2...) custom-call(f32[16,128]{1,0:T(8,128)} %pad_convert_fusion.s_in, ...), custom_call_target="tpu_custom_call" | custom-call | tf_op jit(solution)/shard_map/k1_attention/pallas_call | solution.py:652
  186.0 56.0 %k2_feed.1 = (f32[1024,768]{1,0:T(8,128)}, f32[1024,768]{1,0:T(8,128)}, bf16[2,1024,384]{2,1,0:T(8,128)(2,1)}, bf16[2,2,4,2,4,48,768]{6,5,4,3,2,1,0:T(8,128)(2,1...) custom-call(bf16[1024,768]{1,0:T(8,128)(2,1)} %tok.3, bf16[1024,768]{1,0:T(8,128)(2,1)} %cot.1, ...), custom_call_target="tpu_custom_call" | custom-call | tf_op jit(solution)/shard_map/k2_feed/pallas_call | solution.py:864
  242.0 201.3 %k3_backward.1 = (f32[1024,768]{1,0:T(8,128)}, f32[6,48,768]{2,1,0:T(8,128)}, f32[6,48,512]{2,1,0:T(8,128)}, f32[2,2,48,768]{3,2,1,0:T(8,128)}, f32[3,2,48,128]{3,2,1,0:T(8,128)}, /*index=5*/f32[32,8,128]{2,1,0:T(8,128)}) custom-call(bf16[2,2,4,2,4,48,768]{6,5,4,3,2,1,0:T(8,128)(2,1)} %get-tuple-element.51.def_in, ...), custom_call_target="tpu_custom_call" | custom-call | tf_op jit(solution)/shard_map/k3_backward/pallas_call | solution.py:1417
  443.3 2.0 fusion.9
  445.2 0.7 copy.48
  446.0 0.9 slice_bitcast_fusion
  447.0 0.7 reshape.96
  447.7 0.7 reshape.97
  448.3 0.8 slice.53
  449.2 0.7 dynamic_slice.13
  449.8 0.8 slice_bitcast_fusion.2
  451.2 0.8 slice.54
  452.6 0.7 slice.62
  453.9 1.7 copy.57
  455.7 0.9 copy.58
  456.6 0.8 copy.59
  (20 shorter events, 3.3 us)
Async XLA Ops:
  443.3 10.6 %copy-start = (f32[1024,768]{1,0:T(8,128)S(1)}, f32[1024,768]{1,0:T(8,128)}, u32[]{:S(2)}) copy-start(f32[1024,768]{1,0:T(8,128)} %get-tuple-element.102) | copy-start | bytes 9437188
  453.9 1.8 copy-start.1
  453.9 2.7 copy-start.2

commit v4 on v3

--- a/solution.py
+++ b/solution.py
@@ -384,6 +384,11 @@
     fa.second()
     g.col(*dd(1), 0)
 
+    for i in (1, 2, 3):
+        g.col(*dd(0), i)
+    g.zsend(*dd(1))
+    fa.third()
+
     def arrived(t, f, dev):
         small(t, f, dev).wait_send()
         small(t, f, dev).wait_recv()
@@ -406,10 +411,6 @@
 
     nrm_copy = pltpu.make_async_copy(nrm, nrm_o, tsem.at[4])
     nrm_copy.start()
-    for i in (1, 2, 3):
-        g.col(*dd(0), i)
-    g.zsend(*dd(1))
-    fa.third()
     for zz in range(4):
         g.diag(vo_args[0], vo_args[2], zz)
     g.col(*ll(1), 0)

time: 462 us -> 462 us (level)
  no operation moved by 1% of the time
where the time goes in v4:
time: 462 us; the launch traced here: 458 us
  Pallas kernels  434 us (94%)
  local copies, waits for them, and re-layouts  18.9 us (4%)
    pallas_call x1, Pallas kernels, k3_call(): pl.pallas_call(k3_kernel, out_shape=(sds((ROWS_DEV, D), f32), sds((6, 48,...  201 us
    pallas_call x1, Pallas kernels, k1_call(): pl.pallas_call(k1_kernel, out_shape=(sds((2, 4, 2, 4, 48, HALF), bf16), s...  177 us
    pallas_call x1, Pallas kernels, k2_call(): pl.pallas_call(k2_kernel, out_shape=(sds((ROWS_DEV, D), f32), sds((ROWS_D...  56 us

profile of v4, /device:TPU:0, one launch (start us, length us, event | category | flops | bytes accessed | tf_op | source)
XLA Modules:
  0.0 457.7 jit_solution(18299692773978208169)
XLA Ops:
  0.7 0.9 copy.52
  1.6 1.7 pad_maximum_fusion.ff
  3.2 0.8 stack_reshape.12
  4.0 0.8 stack_reshape.13
  5.5 0.8 stack.37
  6.3 0.7 reshape.85
  7.0 0.8 reshape.86
  7.8 0.7 fusion.7
  9.0 177.0 %k1_attention.1 = (bf16[2,4,2,4,48,384]{5,4,3,2,1,0:T(8,128)(2,1)}, bf16[3,4,2,4,48,768]{5,4,3,2,1,0:T(8,128)(2,1)}, bf16[3,4,2,4,48,512]{5,4,3,2,1,0:T(8,128)(2...) custom-call(f32[16,128]{1,0:T(8,128)} %pad_convert_fusion.s_in, ...), custom_call_target="tpu_custom_call" | custom-call | tf_op jit(solution)/shard_map/k1_attention/pallas_call | solution.py:653
  186.0 56.0 %k2_feed.1 = (f32[1024,768]{1,0:T(8,128)}, f32[1024,768]{1,0:T(8,128)}, bf16[2,1024,384]{2,1,0:T(8,128)(2,1)}, bf16[2,2,4,2,4,48,768]{6,5,4,3,2,1,0:T(8,128)(2,1...) custom-call(bf16[1024,768]{1,0:T(8,128)(2,1)} %tok.3, bf16[1024,768]{1,0:T(8,128)(2,1)} %cot.1, ...), custom_call_target="tpu_custom_call" | custom-call | tf_op jit(solution)/shard_map/k2_feed/pallas_call | solution.py:865
  242.0 201.3 %k3_backward.1 = (f32[1024,768]{1,0:T(8,128)}, f32[6,48,768]{2,1,0:T(8,128)}, f32[6,48,512]{2,1,0:T(8,128)}, f32[2,2,48,768]{3,2,1,0:T(8,128)}, f32[3,2,48,128]{3,2,1,0:T(8,128)}, /*index=5*/f32[32,8,128]{2,1,0:T(8,128)}) custom-call(bf16[2,2,4,2,4,48,768]{6,5,4,3,2,1,0:T(8,128)(2,1)} %get-tuple-element.51.def_in, ...), custom_call_target="tpu_custom_call" | custom-call | tf_op jit(solution)/shard_map/k3_backward/pallas_call | solution.py:1418
  443.3 2.0 fusion.9
  445.2 0.7 copy.48
  446.0 0.9 slice_bitcast_fusion
  447.0 0.7 reshape.96
  447.7 0.7 reshape.97
  448.3 0.8 slice.53
  449.2 0.7 dynamic_slice.13
  449.8 0.8 slice_bitcast_fusion.2
  451.2 0.8 slice.54
  452.6 0.7 slice.62
  453.9 1.7 copy.57
  455.7 0.9 copy.58
  456.6 0.8 copy.59
  (20 shorter events, 3.3 us)
Async XLA Ops:
  443.3 10.6 %copy-start = (f32[1024,768]{1,0:T(8,128)S(1)}, f32[1024,768]{1,0:T(8,128)}, u32[]{:S(2)}) copy-start(f32[1024,768]{1,0:T(8,128)} %get-tuple-element.102) | copy-start | bytes 9437188
  453.9 1.8 copy-start.1
  453.9 2.7 copy-start.2
